TPU v7x, 128 devices: a whole 4x4x4 slice. The times are simulated.
128 devices in a mesh: row: 8 (over x, y_hi), col: 16 (over y_lo, z, core).
Axes of the slice: x: 4, y: 4 (y_hi: 2, y_lo: 2; y = y_hi * 2 + y_lo), z: 4, core: 2. Of those that a mesh axis runs over, the one named last changes fastest.
Arguments:
- tokens: bfloat16 [1024, 6144], P('row', 'col'), may hold values from -6 to 6
- weight_in: bfloat16 [6144, 24576], P('col', 'row'), may hold values from -0.078125 to 0.078125
- weight_out: bfloat16 [24576, 6144], P('row', 'col'), may hold values from -0.0390625 to 0.0390625
- cotangent: bfloat16 [1024, 6144], P('row', 'col'), may hold values from -6 to 6
Outputs:
- output: bfloat16 [1024, 6144], P('row', 'col')
- grad_tokens: bfloat16 [1024, 6144], P('row', 'col')
- grad_in: bfloat16 [6144, 24576], P('col', 'row')
- grad_out: bfloat16 [24576, 6144], P('row', 'col')
All inputs are finite; a program needn't handle non-finite values.
Results may differ from a plain program's by a relative error of at most 0.0049.
Values may be sent and summed in bfloat16 or wider, within the bound.
A program may use at most 128 MiB of HBM per device.

v0:
```python
import jax
import jax.numpy as jnp
from jax import lax
from jax.sharding import PartitionSpec as P


def gelu_tanh(values):
    return jax.nn.gelu(values, approximate=True)


def summed_cols(left_side, right_side, contract):
    row_total = left_side.shape[0] // lax.axis_size("col")

    def partial_term(row_start, row_count):
        return lax.dot_general(
            left_side,
            right_side,
            (((1,), (contract,)), ((), ())),
            preferred_element_type=jnp.float32,
        )

    return lax.psum_scatter(
        partial_term(jnp.int32(0), row_total * lax.axis_size("col")),
        "col",
        scatter_dimension=0,
        tiled=True,
    )


def column_panels(block_in):
    return lax.all_gather(block_in, "col", axis=0, tiled=True)


def summed_rows(left_side, right_side, contract):
    row_total = left_side.shape[0] // lax.axis_size("row")

    def partial_term(row_start, row_count):
        return lax.dot_general(
            left_side,
            right_side,
            (((1,), (contract,)), ((), ())),
            preferred_element_type=jnp.float32,
        )

    return lax.psum_scatter(
        partial_term(jnp.int32(0), row_total * lax.axis_size("row")),
        "row",
        scatter_dimension=0,
        tiled=True,
    )


def local(tokens, weight_in, weight_out, cotangent):
    token_all, cotan_all = (
        lax.all_gather(tokens, "row", axis=0, tiled=True),
        lax.all_gather(cotangent, "row", axis=0, tiled=True),
    )
    hidden = summed_cols(token_all, weight_in, 0)
    activated, pullback = jax.vjp(gelu_tanh, hidden)
    acts_all = column_panels(activated.astype(jnp.bfloat16))
    output = summed_rows(acts_all, weight_out, 0).astype(jnp.bfloat16)
    grad_acts = summed_cols(cotan_all, weight_out, 1)
    grad_all = column_panels(pullback(grad_acts)[0].astype(jnp.bfloat16))
    grad_out = lax.dot_general(
        acts_all, cotan_all, (((0,), (0,)), ((), ())), preferred_element_type=jnp.float32
    ).astype(jnp.bfloat16)
    grad_in = lax.dot_general(
        token_all, grad_all, (((0,), (0,)), ((), ())), preferred_element_type=jnp.float32
    ).astype(jnp.bfloat16)
    grad_tokens = summed_rows(grad_all, weight_in, 1).astype(jnp.bfloat16)
    return (output, grad_tokens, grad_in, grad_out)


def solution(mesh):
    placed = (P("row", "col"), P("col", "row"), P("row", "col"), P("row", "col"))
    return jax.shard_map(
        local,
        mesh=mesh,
        in_specs=placed,
        out_specs=(P("row", "col"), P("row", "col"), P("col", "row"), P("row", "col")),
        check_vma=False,
    )
```

profile of v0, /device:TPU:0, one launch (start us, length us, event | category | flops | bytes accessed | tf_op | source)
XLA Modules:
  0.0 482.5 jit_solution(7322708277229311443)
XLA Ops:
  7.2 0.0 reduce-scatter.5.cloned.1.call-start
  7.2 35.9 %all_gather.12 = bf16[1024,384]{1,0:T(8,128)(2,1)S(1)} all-gather(bf16[128,384]{1,0:T(8,128)(2,1)} %param.4), channel_id=1, replica_groups=mesh['row'=8,'col'=16] {'row'}, dimensions={0}, use_global_device_ids=true | all-gather | bytes 884736 | tf_op jit(solution)/shard_map/all_gather | solution.py:55
  43.1 8.0 %fusion.8 = f32[1024,3072]{1,0:T(8,128)} fusion(bf16[1024,384]{1,0:T(8,128)(2,1)S(1)} %all_gather.12, bf16[384,3072]{1,0:T(8,128)(2,1)} %param.5), kind=kOutput, calls=%fused_computation.13 | convolution fusion | flops 2415919104 | bytes 15728640 | tf_op jit(solution)/shard_map/dot_general | solution.py:15
  51.1 0.0 reduce-scatter.5.cloned.1.call-update
  51.1 0.0 reduce-scatter.9.cloned.1.call-start
  51.2 0.8 copy-done.3
  52.0 36.0 %all_gather.14 = bf16[1024,384]{1,0:T(8,128)(2,1)S(1)} all-gather(bf16[128,384]{1,0:T(8,128)(2,1)S(1)} %copy-done.3), channel_id=1, replica_groups=mesh['row'=8,'col'=16] {'row'}, dimensions={0}, use_global_device_ids=true | all-gather | bytes 884736 | tf_op jit(solution)/shard_map/all_gather | solution.py:56
  88.0 1.0 copy-done.1
  88.9 6.5 %fusion.10 = f32[1024,3072]{1,0:T(8,128)} fusion(bf16[1024,384]{1,0:T(8,128)(2,1)S(1)} %all_gather.14, bf16[3072,384]{1,0:T(8,128)(2,1)S(1)} %copy-done), kind=kOutput, calls=%fused_computation.15 | convolution fusion | flops 2415919104 | bytes 15728640 | tf_op jit(solution)/shard_map/dot_general | solution.py:15
  95.4 0.0 reduce-scatter.9.cloned.1.call-update
  95.4 0.0 all-gather.3.cloned.1.call-start
  95.5 49.3 %reduce-scatter.5.cloned.1.call-done = f32[64,3072]{1,0:T(8,128)} async-done(((f32[1024,3072]{1,0:T(8,128)}), f32[64,3072]{1,0:T(8,128)}) %reduce-scatter.5.cloned.1.call-update) | async-done | bytes 786448 | tf_op jit(solution)/shard_map/reduce_scatter | solution.py:22
  144.8 84.2 %reduce-scatter.9.cloned.1.call-done = f32[64,3072]{1,0:T(8,128)} async-done(((f32[1024,3072]{1,0:T(8,128)}), f32[64,3072]{1,0:T(8,128)}) %reduce-scatter.9.cloned.1.call-update) | async-done | bytes 786448 | tf_op jit(solution)/shard_map/reduce_scatter | solution.py:22
  228.9 2.8 fusion.7
  231.8 0.0 all-gather.3.cloned.1.call-update
  231.8 0.0 all-gather.5.cloned.1.call-start
  231.8 0.5 all-gather.5.cloned.1.call-update
  232.4 0.0 reduce-scatter.7.cloned.1.call-start
  232.4 41.0 %all-gather.3.cloned.1.call-done = bf16[1024,3072]{1,0:T(8,128)(2,1)} async-done(((bf16[64,3072]{1,0:T(8,128)(2,1)}), bf16[1024,3072]{1,0:T(8,128)(2,1)}) %all-gather.3.cloned.1.call-update) | async-done | bytes 6291472 | tf_op jit(solution)/shard_map/all_gather | solution.py:31
  273.4 6.6 %fusion.9 = f32[1024,384]{1,0:T(8,128)} fusion(bf16[1024,3072]{1,0:T(8,128)(2,1)} %all-gather.3.cloned.1.call-done, bf16[3072,384]{1,0:T(8,128)(2,1)S(1)} %copy-done), kind=kOutput, calls=%fused_computation.14 | convolution fusion | flops 2415919104 | bytes 10223616 | tf_op jit(solution)/shard_map/dot_general | solution.py:38
  280.0 0.0 reduce-scatter.7.cloned.1.call-update
  280.0 0.2 reduce-scatter.11.cloned.1.call-start
  280.3 38.5 %all-gather.5.cloned.1.call-done = bf16[1024,3072]{1,0:T(8,128)(2,1)} async-done(((bf16[64,3072]{1,0:T(8,128)(2,1)}), bf16[1024,3072]{1,0:T(8,128)(2,1)}) %all-gather.5.cloned.1.call-update) | async-done | bytes 6291472 | tf_op jit(solution)/shard_map/all_gather | solution.py:31
  318.8 8.0 %fusion.11 = f32[1024,384]{1,0:T(8,128)} fusion(bf16[1024,3072]{1,0:T(8,128)(2,1)} %all-gather.5.cloned.1.call-done, bf16[384,3072]{1,0:T(8,128)(2,1)} %param.5), kind=kOutput, calls=%fused_computation.16 | convolution fusion | flops 2415919104 | bytes 10223616 | tf_op jit(solution)/shard_map/dot_general | solution.py:38
  326.8 0.0 reduce-scatter.11.cloned.1.call-update
  326.9 7.7 %fusion = bf16[384,3072]{0,1:T(8,128)(2,1)} fusion(bf16[1024,3072]{1,0:T(8,128)(2,1)} %all-gather.5.cloned.1.call-done, bf16[1024,384]{1,0:T(8,128)(2,1)S(1)} %all_gather.12), kind=kOutput, calls=%fused_computation.2 | convolution fusion | flops 2417098752 | bytes 9437184 | tf_op jit(solution)/shard_map/dot_general | solution.py:67
  334.5 4.3 copy.8
  338.9 7.7 %convolution_convert_fusion = bf16[3072,384]{1,0:T(8,128)(2,1)} fusion(bf16[1024,3072]{1,0:T(8,128)(2,1)} %all-gather.3.cloned.1.call-done, bf16[1024,384]{1,0:T(8,128)(2,1)S(1)} %copy-done.2), kind=kOutput, calls=%fused_computation | convolution fusion | flops 2417098752 | bytes 9437184 | tf_op jit(solution)/shard_map/dot_general | solution.py:64
  346.6 50.8 %reduce-scatter.7.cloned.1.call-done = f32[128,384]{1,0:T(8,128)} async-done(((f32[1024,384]{1,0:T(8,128)}), f32[128,384]{1,0:T(8,128)}) %reduce-scatter.7.cloned.1.call-update) | async-done | bytes 196624 | tf_op jit(solution)/shard_map/reduce_scatter | solution.py:45
  397.4 1.6 convert_element_type.22
  399.0 75.1 %reduce-scatter.11.cloned.1.call-done = f32[128,384]{1,0:T(8,128)} async-done(((f32[1024,384]{1,0:T(8,128)}), f32[128,384]{1,0:T(8,128)}) %reduce-scatter.11.cloned.1.call-update) | async-done | bytes 196624 | tf_op jit(solution)/shard_map/reduce_scatter | solution.py:45
  474.1 1.6 convert_element_type.24
  (6 shorter events, 0.0 us)
Async XLA Ops:
  7.2 81.8 %copy-start = (bf16[3072,384]{1,0:T(8,128)(2,1)S(1)}, bf16[3072,384]{1,0:T(8,128)(2,1)}, u32[]{:S(2)}) copy-start(bf16[3072,384]{1,0:T(8,128)(2,1)} %param.6) | copy-start | bytes 7077892
  7.2 137.6 %reduce-scatter.5.cloned.1.call-start = ((), (), s32[]{:S(2)}) async-start(), calls=%async_computation.4 | async-start | bytes 13369344 | tf_op jit(solution)/shard_map/reduce_scatter | solution.py:22
  51.1 0.9 copy-start.3
  51.1 177.8 %reduce-scatter.9.cloned.1.call-start = ((), (), s32[]{:S(2)}) async-start(), calls=%async_computation.7 | async-start | bytes 13369344 | tf_op jit(solution)/shard_map/reduce_scatter | solution.py:22
  88.0 1.0 copy-start.1
  95.4 177.9 %all-gather.3.cloned.1.call-start = ((), (), s32[]{:S(2)}) async-start(), calls=%async_computation.5 | async-start | bytes 6684672 | tf_op jit(solution)/shard_map/all_gather | solution.py:31
  231.8 87.0 %all-gather.5.cloned.1.call-start = ((), (), s32[]{:S(2)}) async-start(), calls=%async_computation.8 | async-start | bytes 6684672 | tf_op jit(solution)/shard_map/all_gather | solution.py:31
  232.4 165.0 %reduce-scatter.7.cloned.1.call-start = ((), (), s32[]{:S(2)}) async-start(), calls=%async_computation.6 | async-start | bytes 1769472 | tf_op jit(solution)/shard_map/reduce_scatter | solution.py:45
  280.0 194.0 %reduce-scatter.11.cloned.1.call-start = ((), (), s32[]{:S(2)}) async-start(), calls=%async_computation.9 | async-start | bytes 1769472 | tf_op jit(solution)/shard_map/reduce_scatter | solution.py:45
  334.5 4.3 copy-start.2
Sparse Core Ops, SparseCore 0:
  51.2 93.4 reduce-scatter.4
  147.2 81.7 reduce-scatter.8
  231.9 41.4 all-gather.2
  275.5 43.2 all-gather.4
  322.4 74.9 reduce-scatter.6
  401.0 73.0 reduce-scatter.10
where the time goes:
time: 483 us; the launch traced here: 482 us
  waiting for transfers between devices  339 us (70%)
  blocking collectives  71.9 us (15%)
  matrix products  44.5 us (9%)
  between operations  14.1 us (3%)
  local copies, waits for them, and re-layouts  6.13 us (1%)
  other arithmetic  5.97 us (1%)
    reduce_scatter x2, waiting for transfers between devices, summed_cols(): lax.psum_scatter(partial_term(jnp.int32(0), row_total * lax.axis_size('co...  133 us
    reduce_scatter x2, waiting for transfers between devices, summed_rows(): lax.psum_scatter(partial_term(jnp.int32(0), row_total * lax.axis_size('ro...  126 us
    all_gather x2, waiting for transfers between devices, column_panels(): return lax.all_gather(block_in, 'col', axis=0, tiled=True)  79.5 us
    all_gather x1, blocking collectives, local(): lax.all_gather(cotangent, 'row', axis=0, tiled=True)  36 us
    all_gather x1, blocking collectives, local(): lax.all_gather(tokens, 'row', axis=0, tiled=True)  35.9 us
    dot_general x4, matrix products, partial_term(): lax.dot_general(left_side, right_side, (((1,), (contract,)), ((), ())), p...  29.2 us
  transfers between devices with their start and end apart: 6, of which 6 were waited for; matrix products, arithmetic and copies ran while one was open for 9% of the time, Pallas kernels for 0%

commit v1 on v0

v1 whole, which is shorter than its diff:
```python
import functools

import jax
import jax.numpy as jnp
from jax import lax
from jax.experimental import pallas as pl
from jax.experimental.pallas import tpu as pltpu
from jax.sharding import PartitionSpec as P

F32 = jnp.float32
BF16 = jnp.bfloat16

TOK = 1024
BLK = 128
DC = 384
DP = 2 * DC
FH = 1536
FA = 768
FB = FH - FA

COPIES = 128
C_GELU = 0.7978845608028654
C_CUBE = 0.044715


def row_loop(rows, chunk, body):
    def step(i, carry):
        body(pl.multiple_of(i * chunk, chunk))
        return carry

    lax.fori_loop(0, rows // chunk, step, 0)


def tiles(count, body):
    def step(i, carry):
        body(i)
        return carry

    lax.fori_loop(0, count, step, 0)


class Links:
    def __init__(self, send, recv):
        self.send, self.recv, self.used, self.started = send, recv, 0, []
        row, col = lax.axis_index("row"), lax.axis_index("col")
        self.x, self.yh = row // 2, row % 2
        self.yl, self.z, self.k = col // 8, (col // 2) % 4, col % 2

    def device(self, **moved):
        at = {n: moved.get(n, getattr(self, n)) for n in ("x", "yh", "yl", "z", "k")}
        return (at["x"] * 2 + at["yh"], at["yl"] * 8 + at["z"] * 2 + at["k"])

    def ring(self, axis, step):
        return self.device(**{axis: lax.rem(getattr(self, axis) + step + 4, 4)})

    def other(self, axis):
        return self.device(**{axis: 1 - getattr(self, axis)})

    def copy(self, src, dst, device):
        i = self.used
        self.used += 1
        c = pltpu.make_async_remote_copy(
            src_ref=src,
            dst_ref=dst,
            send_sem=self.send.at[i],
            recv_sem=self.recv.at[i],
            device_id=device,
            device_id_type=pl.DeviceIdType.MESH,
        )
        c.start()
        self.started.append(c)
        return c

    def place(self, axis, step):
        return lax.rem(getattr(self, axis) + step + 4, 4)


def rows_of(place, member, count=BLK, skip=0):
    return pl.ds(pl.multiple_of(place * (2 * BLK) + member * BLK + skip, 16), count)


class GatherRingLast:
    def __init__(self, links, ring, pair, buf, cols):
        self.l, self.ring, self.pair, self.buf, self.cols = links, ring, pair, buf, cols
        self.me, self.mine = getattr(links, ring), getattr(links, pair)

    def at(self, step, member):
        return self.buf.at[rows_of(self.l.place(self.ring, step), member), self.cols]

    def send(self, ref, device):
        return self.l.copy(ref, ref, device)

    def start(self):
        own = self.at(0, self.mine)
        self.y = self.send(own, self.l.other(self.pair))
        self.own_p = self.send(own, self.l.ring(self.ring, 1))
        self.own_m = self.send(own, self.l.ring(self.ring, -1))

    def second(self):
        self.y.wait_recv()
        theirs = self.at(0, 1 - self.mine)
        self.oth_p = self.send(theirs, self.l.ring(self.ring, 1))
        self.oth_m = self.send(theirs, self.l.ring(self.ring, -1))

    def third(self):
        self.own_p.wait_recv()
        self.far_p = self.send(self.at(-1, self.mine), self.l.ring(self.ring, 1))
        self.own_m.wait_recv()
        self.oth_m.wait_recv()
        self.far_m = self.send(self.at(1, 1 - self.mine), self.l.ring(self.ring, -1))
        self.oth_p.wait_recv()

    def finish(self):
        self.far_p.wait_recv()
        self.far_m.wait_recv()


class GatherRingFirst:
    def __init__(self, links, ring, pair, buf, cols):
        self.l, self.ring, self.pair, self.buf, self.cols = links, ring, pair, buf, cols
        self.mine = getattr(links, pair)

    def at(self, step, count=BLK, skip=0):
        return self.buf.at[rows_of(self.l.place(self.ring, step), self.mine, count, skip), self.cols]

    def send(self, ref, device):
        return self.l.copy(ref, ref, device)

    def across(self, ref):
        return self.send(ref, self.l.other(self.pair))

    def start(self):
        own = self.at(0)
        self.own_p = self.send(own, self.l.ring(self.ring, 1))
        self.own_m = self.send(own, self.l.ring(self.ring, -1))
        self.y0 = self.across(own)

    def second(self):
        self.own_p.wait_recv()
        self.far_p = self.send(self.at(-1, BLK // 2), self.l.ring(self.ring, 1))
        self.yp = self.across(self.at(-1))
        self.own_m.wait_recv()
        self.far_m = self.send(self.at(1, BLK // 2, BLK // 2), self.l.ring(self.ring, -1))
        self.ym = self.across(self.at(1))

    def third(self):
        self.far_p.wait_recv()
        self.yfp = self.across(self.at(2, BLK // 2))
        self.far_m.wait_recv()
        self.yfm = self.across(self.at(2, BLK // 2, BLK // 2))

    def near(self):
        for c in (self.y0, self.yp, self.ym):
            c.wait_recv()

    def finish(self):
        self.yfp.wait_recv()
        self.yfm.wait_recv()


class ReduceRingFirst:
    def __init__(self, links, ring, pair, part, out, col, out_col, width, slots):
        self.l, self.ring, self.pair = links, ring, pair
        self.part, self.out, self.col, self.width, self.slots = part, out, col, width, slots
        self.out_cols = pl.ds(out_col, width)
        self.mine = getattr(links, pair)

    def rows(self, step, member):
        return rows_of(self.l.place(self.ring, step), member)

    def block(self, step, member):
        return self.out.at[self.rows(step, member), self.out_cols]

    def sent(self, step):
        l = self.l
        if step == 2:
            self.p2 = l.copy(self.block(2, 0), self.slots.at[0], l.ring(self.ring, 1))
            self.m2 = l.copy(self.block(2, 1), self.slots.at[1], l.ring(self.ring, -1))
        elif step == 1:
            self.p1 = l.copy(self.block(1, 1), self.slots.at[2], l.ring(self.ring, 1))
        elif step == 3:
            self.m1 = l.copy(self.block(-1, 0), self.slots.at[3], l.ring(self.ring, -1))

    def add(self, dst, rows_start, *slots):
        def body(r):
            total = self.part[pl.ds(rows_start + r, 32), pl.ds(self.col, self.width)]
            for s in slots:
                total = total + self.slots[s, pl.ds(r, 32), :].astype(F32)
            dst(r, total)

        row_loop(BLK, 32, body)

    def start_of(self, step, member):
        return pl.multiple_of(self.l.place(self.ring, step) * (2 * BLK) + member * BLK, BLK)

    def to_slot(self, slot):
        def put(r, total):
            self.slots[slot, pl.ds(r, 32), :] = total.astype(BF16)

        return put

    def combine(self):
        l = self.l
        self.p2.wait_recv()
        self.add(self.to_slot(7), self.start_of(1, 0), 0)
        self.pc = l.copy(self.slots.at[7], self.slots.at[4], l.ring(self.ring, 1))
        self.m2.wait_recv()
        self.add(self.to_slot(8), self.start_of(-1, 1), 1)
        self.mc = l.copy(self.slots.at[8], self.slots.at[5], l.ring(self.ring, -1))

    def across(self):
        for c in (self.p1, self.m1, self.pc, self.mc):
            c.wait_recv()
        for member, slots in ((0, (4, 3)), (1, (2, 5))):
            start = self.start_of(0, member)

            def put(r, total, start=start):
                self.part[pl.ds(start + r, 32), pl.ds(self.col, self.width)] = total

            self.add(put, start, *slots)
        self.add(self.to_slot(9), self.start_of(0, 1 - self.mine))
        self.y = self.l.copy(self.slots.at[9], self.slots.at[6], self.l.other(self.pair))

    def finish(self, put):
        self.y.wait_recv()
        self.add(put, self.start_of(0, self.mine), 6)


class ReducePairFirst:
    def __init__(self, links, ring, pair, part, out, col, width, slots, halves):
        self.l, self.ring, self.pair = links, ring, pair
        self.part, self.out, self.col, self.width = part, out, col, width
        self.slots, self.halves = slots, halves
        self.mine = getattr(links, pair)
        self.y = {}

    def sent(self, step):
        rows = rows_of(self.l.place(self.ring, step), 1 - self.mine)
        block = self.out.at[rows, pl.ds(self.col, self.width)]
        self.y[step] = self.l.copy(block, self.slots.at[step], self.l.other(self.pair))

    def add(self, dst, step, skip, count, *halves):
        start = pl.multiple_of(self.l.place(self.ring, step) * (2 * BLK) + self.mine * BLK + skip, 64)

        def body(r):
            total = self.part[pl.ds(start + r, 32), pl.ds(self.col, self.width)]
            total = total + self.slots[step, pl.ds(skip + r, 32), :].astype(F32)
            for h in halves:
                total = total + self.halves[h, pl.ds(r, 32), :].astype(F32)
            dst(r, total)

        row_loop(count, 32, body)

    def to_half(self, half):
        def put(r, total):
            self.halves[half, pl.ds(r, 32), :] = total.astype(BF16)

        return put

    def ring_copy(self, src, dst, step):
        return self.l.copy(src, self.halves.at[dst], self.l.ring(self.ring, step))

    def pairs(self):
        half = BLK // 2
        self.y[2].wait_recv()

        def put(r, total):
            self.slots[4, pl.ds(r, 32), :] = total.astype(BF16)

        self.add(put, 2, 0, BLK)
        self.p2 = self.ring_copy(self.slots.at[4, pl.ds(0, half)], 0, 1)
        self.m2 = self.ring_copy(self.slots.at[4, pl.ds(half, half)], 1, -1)
        self.y[1].wait_recv()
        self.add(self.to_half(6), 1, half, half)
        self.p1 = self.ring_copy(self.halves.at[6], 2, 1)
        self.y[3].wait_recv()
        self.add(self.to_half(7), 3, 0, half)
        self.m1 = self.ring_copy(self.halves.at[7], 3, -1)

    def combine(self):
        half = BLK // 2
        self.p2.wait_recv()
        self.add(self.to_half(8), 1, 0, half, 0)
        self.pc = self.ring_copy(self.halves.at[8], 4, 1)
        self.m2.wait_recv()
        self.add(self.to_half(9), 3, half, half, 1)
        self.mc = self.ring_copy(self.halves.at[9], 5, -1)

    def finish(self, put):
        half = BLK // 2
        for c in (self.y[0], self.p1, self.m1, self.pc, self.mc):
            c.wait_recv()
        self.add(put, 0, 0, half, 4, 3)
        self.add(lambda r, total: put(half + r, total), 0, half, half, 2, 5)


def dot(a, b, left, right):
    return lax.dot_general(a, b, (((left,), (right,)), ((), ())), preferred_element_type=F32)


def kernel(
    tok_in, wi_in, wo_in, cot_in,
    out_ref, gt_ref, gi_ref, go_ref,
    tok, cot, wi, wo,
    part_h, part_g, send_h, send_g,
    ra_h, ra_g, rb_h, rb_g, rh_h, rh_g,
    hid, gacts, acts, ghid,
    sib_out, sib_in, rbuf, rd,
    gi, go, final,
    send, recv, local,
):
    l = Links(send, recv)
    k = l.k
    sib = l.other("k")

    barrier = pltpu.get_barrier_semaphore()
    near = [sib, l.other("yl"), l.other("yh")]
    near += [l.ring(a, s) for a in ("z", "x") for s in (1, -1)]
    for d in near:
        pl.semaphore_signal(barrier, inc=1, device_id=d, device_id_type=pl.DeviceIdType.MESH)

    my_d = pl.ds(pl.multiple_of(k * DC, 128), DC)
    its_d = pl.ds(pl.multiple_of((1 - k) * DC, 128), DC)
    my_f = pl.ds(pl.multiple_of(k * FH, 128), FH)
    its_f = pl.ds(pl.multiple_of((1 - k) * FH, 128), FH)
    own_rows = rows_of(l.x, l.yh)

    loads = [
        pltpu.make_async_copy(tok_in, tok.at[own_rows, my_d], local.at[0]),
        pltpu.make_async_copy(cot_in, cot.at[own_rows, my_d], local.at[1]),
        pltpu.make_async_copy(wi_in.at[:, my_f], wi.at[my_d], local.at[2]),
        pltpu.make_async_copy(wo_in.at[my_f], wo.at[:, my_d], local.at[3]),
    ]
    for c in loads:
        c.start()
    pl.semaphore_wait(barrier, len(near))

    gather_tok = GatherRingLast(l, "x", "yh", tok, my_d)
    gather_cot = GatherRingLast(l, "x", "yh", cot, my_d)
    loads[0].wait()
    gather_tok.start()
    wi_copy = l.copy(wi_in.at[:, its_f], wi.at[my_d], sib)
    loads[1].wait()
    gather_cot.start()
    wo_copy = l.copy(wo_in.at[its_f], wo.at[:, my_d], sib)

    def share(buf, step):
        ref = buf.at[pl.ds(pl.multiple_of(l.place("x", step) * (2 * BLK), 2 * BLK), 2 * BLK), my_d]
        return l.copy(ref, ref, sib)

    shared_tok, shared_cot = [], []
    gather_tok.second()
    shared_tok.append(share(tok, 0))
    gather_tok.third()
    shared_tok += [share(tok, 1), share(tok, -1)]
    gather_cot.second()
    shared_cot.append(share(cot, 0))
    gather_tok.finish()
    shared_tok.append(share(tok, 2))
    for c in shared_tok:
        c.wait_recv()
    loads[2].wait()
    wi_copy.wait_recv()

    ring = [
        ReduceRingFirst(l, "z", "yl", part, out, 0, 0, FA, slots)
        for part, out, slots in ((part_h, send_h, ra_h), (part_g, send_g, ra_g))
    ]
    pair = [
        ReducePairFirst(l, "z", "yl", part, out, FA, FB, slots, halves)
        for part, out, slots, halves in ((part_h, send_h, rb_h, rh_h), (part_g, send_g, rb_g, rh_g))
    ]

    def pair_rows(axis, step):
        return pl.ds(pl.multiple_of(l.place(axis, step) * (2 * BLK), 2 * BLK), 2 * BLK)

    def partial_hidden(step):
        rows = pair_rows("z", step)

        def tile(n):
            cols = pl.ds(pl.multiple_of(n * 512, 512), 512)
            total = dot(tok[rows, :], wi[:, cols], 1, 0)
            part_h[rows, cols] = total
            send_h[rows, cols] = total.astype(BF16)

        tiles(FH // 512, tile)
        ring[0].sent(step)
        pair[0].sent(step)

    def partial_grad(step):
        rows = pair_rows("z", step)

        def tile(n):
            cols = pl.ds(pl.multiple_of(n * 512, 512), 512)
            total = dot(cot[rows, :], wo[cols, :], 1, 1)
            part_g[rows, cols] = total
            send_g[rows, cols] = total.astype(BF16)

        tiles(FH // 512, tile)
        ring[1].sent(step)
        pair[1].sent(step)

    for step in (2, 1, 3, 0):
        partial_hidden(step)
    gather_cot.third()
    shared_cot += [share(cot, 1), share(cot, -1)]
    gather_cot.finish()
    shared_cot.append(share(cot, 2))

    ring[0].combine()
    pair[0].pairs()
    for c in shared_cot:
        c.wait_recv()
    loads[3].wait()
    wo_copy.wait_recv()
    partial_grad(2)
    pair[0].combine()
    ring[0].across()
    for step in (1, 3, 0):
        partial_grad(step)

    def put_into(buf, col, width):
        def put(r, total):
            buf[pl.ds(r, 32), pl.ds(col, width)] = total

        return put

    own = pl.multiple_of(l.z * (2 * BLK) + l.yl * BLK, BLK)
    ring[0].finish(put_into(hid, 0, FA))
    pair[0].finish(put_into(hid, FA, FB))

    def activate(r):
        h = hid[pl.ds(r, 16), :]
        t = jnp.tanh(C_GELU * (h + C_CUBE * (h * h * h)))
        acts[pl.ds(own + r, 16), :] = (0.5 * h * (1.0 + t)).astype(BF16)

    row_loop(BLK, 16, activate)
    acts_a = GatherRingLast(l, "z", "yl", acts, pl.ds(0, FA))
    acts_b = GatherRingFirst(l, "z", "yl", acts, pl.ds(FA, FB))
    acts_a.start()
    acts_b.start()

    ring[1].combine()
    pair[1].pairs()
    acts_a.second()
    pair[1].combine()
    ring[1].across()
    acts_b.second()
    acts_a.third()
    acts_b.third()
    ring[1].finish(put_into(gacts, 0, FA))
    pair[1].finish(put_into(gacts, FA, FB))

    def pull(r):
        h = hid[pl.ds(r, 16), :]
        square = h * h
        t = jnp.tanh(C_GELU * (h + C_CUBE * (square * h)))
        slope = 0.5 * (1.0 + t) + (0.5 * C_GELU) * h * (1.0 - t * t) * (1.0 + 3.0 * C_CUBE * square)
        ghid[pl.ds(own + r, 16), :] = (gacts[pl.ds(r, 16), :] * slope).astype(BF16)

    row_loop(BLK, 16, pull)
    ghid_a = GatherRingLast(l, "z", "yl", ghid, pl.ds(0, FA))
    ghid_b = GatherRingFirst(l, "z", "yl", ghid, pl.ds(FA, FB))
    ghid_a.start()
    ghid_b.start()

    acts_b.near()
    acts_a.finish()
    acts_b.finish()

    out_pair = ReduceRingFirst(l, "x", "yh", part_h, rbuf.at[0], DP, 0, DC, rd.at[0])
    gt_pair = ReduceRingFirst(l, "x", "yh", part_g, rbuf.at[1], DP, 0, DC, rd.at[1])

    def project(which, part, lhs, weight, right, axis, step):
        rows = pair_rows(axis, step)
        part[rows, pl.ds(0, DP)] = dot(lhs[rows, :], weight[...], 1, right)
        start = pl.multiple_of(l.place(axis, step) * (2 * BLK), 2 * BLK)

        def cast(r):
            sib_out[which, pl.ds(start + r, 32), :] = part[pl.ds(start + r, 32), its_d].astype(BF16)

        row_loop(2 * BLK, 32, cast)
        return l.copy(sib_out.at[which, rows], sib_in.at[which, rows], sib)

    def merge(which, part, copy, step):
        copy.wait_recv()
        start = pl.multiple_of(l.place("x", step) * (2 * BLK), 2 * BLK)

        def body(r):
            at = pl.ds(start + r, 32)
            total = part[at, my_d] + sib_in[which, at, :].astype(F32)
            part[at, pl.ds(DP, DC)] = total
            rbuf[which, at, :] = total.astype(BF16)

        row_loop(2 * BLK, 32, body)

    steps = (2, 1, 3, 0)
    sent_out = [project(0, part_h, acts, wo, 0, "x", s) for s in steps[:2]]
    ghid_a.second()
    ghid_b.second()
    sent_out += [project(0, part_h, acts, wo, 0, "x", s) for s in steps[2:]]
    for s, c in zip(steps, sent_out):
        merge(0, part_h, c, s)
        out_pair.sent(s)
    ghid_a.third()
    ghid_b.third()

    def weight_grad_out(m):
        cols = pl.ds(pl.multiple_of(m * 256, 256), 256)
        go[cols, :] = dot(acts[:, cols], cot[...], 0, 0).astype(BF16)

    tiles(FH // 256, weight_grad_out)
    go_own = pltpu.make_async_copy(go.at[:, my_d], go_ref.at[my_f], local.at[4])
    go_own.start()
    go_sib = l.copy(go.at[:, its_d], go_ref.at[my_f], sib)

    out_pair.combine()
    out_pair.across()

    ghid_b.near()
    ghid_a.finish()
    ghid_b.finish()
    sent_gt = [project(1, part_g, ghid, wi, 1, "x", s) for s in steps]
    for s, c in zip(steps, sent_gt):
        merge(1, part_g, c, s)
        gt_pair.sent(s)

    def put_final(which):
        def put(r, total):
            final[which, pl.ds(r, 32), :] = total.astype(BF16)

        return put

    out_pair.finish(put_final(0))
    out_own = pltpu.make_async_copy(final.at[0], out_ref, local.at[5])
    out_own.start()

    def weight_grad_in(m):
        cols = pl.ds(pl.multiple_of(m * 256, 256), 256)
        gi[cols, :] = dot(tok[:, cols], ghid[...], 0, 0).astype(BF16)

    gt_pair.combine()
    tiles(DP // 256, weight_grad_in)
    gi_own = pltpu.make_async_copy(gi.at[my_d], gi_ref.at[:, my_f], local.at[6])
    gi_own.start()
    gi_sib = l.copy(gi.at[its_d], gi_ref.at[:, my_f], sib)
    gt_pair.across()
    gt_pair.finish(put_final(1))
    gt_own = pltpu.make_async_copy(final.at[1], gt_ref, local.at[7])
    gt_own.start()

    go_sib.wait_recv()
    gi_sib.wait_recv()
    for c in (go_own, out_own, gi_own, gt_own):
        c.wait()
    for c in l.started:
        c.wait_send()


def local(tokens, weight_in, weight_out, cotangent):
    any_space = pl.BlockSpec(memory_space=pl.ANY)
    shape = jax.ShapeDtypeStruct
    vmem = pltpu.VMEM
    return pl.pallas_call(
        kernel,
        out_shape=(
            shape((BLK, DC), BF16),
            shape((BLK, DC), BF16),
            shape((DC, 2 * FH), BF16),
            shape((2 * FH, DC), BF16),
        ),
        in_specs=[any_space] * 4,
        out_specs=(any_space,) * 4,
        scratch_shapes=[
            vmem((TOK, DP), BF16), vmem((TOK, DP), BF16), vmem((DP, FH), BF16), vmem((FH, DP), BF16),
            vmem((TOK, FH), F32), vmem((TOK, FH), F32), vmem((TOK, FH), BF16), vmem((TOK, FH), BF16),
            vmem((10, BLK, FA), BF16), vmem((10, BLK, FA), BF16),
            vmem((5, BLK, FB), BF16), vmem((5, BLK, FB), BF16),
            vmem((10, BLK // 2, FB), BF16), vmem((10, BLK // 2, FB), BF16),
            vmem((BLK, FH), F32), vmem((BLK, FH), F32), vmem((TOK, FH), BF16), vmem((TOK, FH), BF16),
            vmem((2, TOK, DC), BF16), vmem((2, TOK, DC), BF16), vmem((2, TOK, DC), BF16),
            vmem((2, 10, BLK, DC), BF16),
            vmem((DP, FH), BF16), vmem((FH, DP), BF16), vmem((2, BLK, DC), BF16),
            pltpu.SemaphoreType.DMA((COPIES,)), pltpu.SemaphoreType.DMA((COPIES,)),
            pltpu.SemaphoreType.DMA((8,)),
        ],
        compiler_params=pltpu.CompilerParams(
            collective_id=0, has_side_effects=True, vmem_limit_bytes=60 * 1024 * 1024
        ),
        cost_estimate=pl.CostEstimate(flops=14_500_000_000, bytes_accessed=12_000_000, transcendentals=400_000),
    )(tokens, weight_in, weight_out, cotangent)


def solution(mesh):
    placed = (P("row", "col"), P("col", "row"), P("row", "col"), P("row", "col"))
    return jax.shard_map(
        local,
        mesh=mesh,
        in_specs=placed,
        out_specs=(P("row", "col"), P("row", "col"), P("col", "row"), P("row", "col")),
        check_vma=False,
    )
```

time: 483 us -> 139 us (0.29)
  waiting for transfers between devices: 339 us -> 0 us
  Pallas kernels: 0 us -> 129 us
  blocking collectives: 71.9 us -> 0 us
  matrix products: 44.5 us -> 0 us
  between operations: 14.1 us -> 0.64 us
  other arithmetic: 5.97 us -> 0 us
    reduce_scatter x4 -> x0, waiting for transfers between devices: 259 us -> none  [the longest x2 133 us: summed_cols(): lax.psum_scatter(partial_term(jnp.int32(0), row_total * lax.axis_size('co...]
    pallas_call x0 -> x1, Pallas kernels: none -> 129 us  [local(): pl.pallas_call(kernel, out_shape=(shape((BLK, DC), BF16), shape((BLK, DC)...]
    all_gather x2 -> x0, waiting for transfers between devices: 79.5 us -> none  [column_panels(): return lax.all_gather(block_in, 'col', axis=0, tiled=True)]
    all_gather x2 -> x0, blocking collectives: 71.9 us -> none  [the longest x1 36 us: local(): lax.all_gather(cotangent, 'row', axis=0, tiled=True)]
    dot_general x6 -> x0, matrix products: 44.5 us -> none  [the longest x4 29.2 us: partial_term(): lax.dot_general(left_side, right_side, (((1,), (contract,)), ((), ())), p...]
    convert_element_type x3 -> x0, other arithmetic: 5.97 us -> none  [the longest x1 2.81 us: local(): grad_all = column_panels(pullback(grad_acts)[0].astype(jnp.bfloat16))]
  transfers between devices with their start and end apart: 6 -> 0, of which waited for: 6 -> 0; matrix products, arithmetic and copies ran while one was open for 9% -> 0% of each run, Pallas kernels for 0% -> 0%
where the time goes in v1:
time: 139 us; the launch traced here: 138 us
  Pallas kernels  129 us (93%)
  local copies, waits for them, and re-layouts  7.87 us (6%)
    pallas_call x1, Pallas kernels, local(): pl.pallas_call(kernel, out_shape=(shape((BLK, DC), BF16), shape((BLK, DC)...  129 us
    unnamed x6, local copies, waits for them, and re-layouts  7.87 us

profile of v1, /device:TPU:0, one launch (start us, length us, event | category | flops | bytes accessed | tf_op | source)
XLA Modules:
  0.0 138.0 jit_solution(13272878006737185422)
XLA Ops:
  0.6 129.5 %shard_map.75 = (bf16[128,384]{1,0:T(8,128)(2,1)}, bf16[128,384]{1,0:T(8,128)(2,1)}, bf16[384,3072]{1,0:T(8,128)(2,1)}, bf16[3072,384]{1,0:T(8,128)(2,1)}) custom-call(bf16[128,384]{1,0:T(8,128)(2,1)} %tok_in.1, bf16[384,3072]{1,0:T(8,128)(2,1)} %wi_in.1, bf16[3072,384]{1,0:T(8,128)(2,1)} %wo_in.1, bf16[128,384]{1,0:T(8,128)(2,1)} %cot_in.1), custom_call_target="tpu_custom_call" | custom-call | flops 14499999744 | bytes 12000000 | tf_op jit(solution)/shard_map/pallas_call | solution.py:564
  130.1 1.5 %copy.12 = bf16[128,384]{1,0:T(8,128)(2,1)} copy(bf16[128,384]{1,0:T(8,128)(2,1)} %get-tuple-element.8) | data formatting | bytes 196608
  131.6 1.5 %copy.13 = bf16[128,384]{1,0:T(8,128)(2,1)} copy(bf16[128,384]{1,0:T(8,128)(2,1)} %get-tuple-element.9) | data formatting | bytes 196608
  133.2 0.0 copy-start
  133.2 3.4 %copy.14 = bf16[384,3072]{1,0:T(8,128)(2,1)} copy(bf16[384,3072]{1,0:T(8,128)(2,1)} %get-tuple-element.10) | data formatting | bytes 4718592
  136.6 0.0 copy-done
  136.6 1.4 %copy.15 = bf16[3072,384]{1,0:T(8,128)(2,1)} copy(bf16[3072,384]{1,0:T(8,128)(2,1)S(1)} %copy-done) | data formatting | bytes 4718592
Async XLA Ops:
  133.2 3.4 %copy-start = (bf16[3072,384]{1,0:T(8,128)(2,1)S(1)}, bf16[3072,384]{1,0:T(8,128)(2,1)}, u32[]{:S(2)}) copy-start(bf16[3072,384]{1,0:T(8,128)(2,1)} %get-tuple-element.11) | copy-start | bytes 7077892

commit v2 on v1

--- a/solution.py
+++ b/solution.py
@@ -15,7 +15,7 @@
 DC = 384
 DP = 2 * DC
 FH = 1536
-FA = 768
+FA = 896
 FB = FH - FA
 
 COPIES = 128
@@ -341,8 +341,6 @@
     gather_tok.start()
     wi_copy = l.copy(wi_in.at[:, its_f], wi.at[my_d], sib)
     loads[1].wait()
-    gather_cot.start()
-    wo_copy = l.copy(wo_in.at[its_f], wo.at[:, my_d], sib)
 
     def share(buf, step):
         ref = buf.at[pl.ds(pl.multiple_of(l.place("x", step) * (2 * BLK), 2 * BLK), 2 * BLK), my_d]
@@ -353,8 +351,8 @@
     shared_tok.append(share(tok, 0))
     gather_tok.third()
     shared_tok += [share(tok, 1), share(tok, -1)]
-    gather_cot.second()
-    shared_cot.append(share(cot, 0))
+    gather_cot.start()
+    wo_copy = l.copy(wo_in.at[its_f], wo.at[:, my_d], sib)
     gather_tok.finish()
     shared_tok.append(share(tok, 2))
     for c in shared_tok:
@@ -400,7 +398,10 @@
         ring[1].sent(step)
         pair[1].sent(step)
 
-    for step in (2, 1, 3, 0):
+    partial_hidden(2)
+    gather_cot.second()
+    shared_cot.append(share(cot, 0))
+    for step in (1, 3, 0):
         partial_hidden(step)
     gather_cot.third()
     shared_cot += [share(cot, 1), share(cot, -1)]
@@ -557,7 +558,35 @@
         c.wait_send()
 
 
+def hand_over(*refs):
+    sems = refs[-1]
+    copies = []
+    for src, dst in zip(refs[:4], refs[4:8]):
+        parts = 4 if src.shape[0] > BLK else 1
+        rows = src.shape[0] // parts
+        for p in range(parts):
+            at = pl.ds(p * rows, rows)
+            copies.append(pltpu.make_async_copy(src.at[at], dst.at[at], sems.at[len(copies)]))
+    for c in copies:
+        c.start()
+    for c in copies:
+        c.wait()
+
+
 def local(tokens, weight_in, weight_out, cotangent):
+    results = block(tokens, weight_in, weight_out, cotangent)
+    any_space = pl.BlockSpec(memory_space=pl.ANY)
+    return pl.pallas_call(
+        hand_over,
+        out_shape=tuple(jax.ShapeDtypeStruct(r.shape, r.dtype) for r in results),
+        in_specs=[any_space] * 4,
+        out_specs=(any_space,) * 4,
+        scratch_shapes=[pltpu.SemaphoreType.DMA((10,))],
+        compiler_params=pltpu.CompilerParams(vmem_limit_bytes=60 * 1024 * 1024),
+    )(*results)
+
+
+def block(tokens, weight_in, weight_out, cotangent):
     any_space = pl.BlockSpec(memory_space=pl.ANY)
     shape = jax.ShapeDtypeStruct
     vmem = pltpu.VMEM

time: 139 us -> 279 us (2.01)
  Pallas kernels: 129 us -> 278 us
  local copies, waits for them, and re-layouts: 7.87 us -> 0 us
    pallas_call x1 -> x2, Pallas kernels: 129 us -> 278 us  [the longest x1 150 us: local(): pl.pallas_call(hand_over, out_shape=tuple((jax.ShapeDtypeStruct(r.shape,...]
    unnamed x6 -> x0, local copies, waits for them, and re-layouts: 7.87 us -> none
where the time goes in v2:
time: 279 us
  Pallas kernels  278 us (100%)
    pallas_call x1, Pallas kernels, local(): pl.pallas_call(hand_over, out_shape=tuple((jax.ShapeDtypeStruct(r.shape,...  150 us
    pallas_call x1, Pallas kernels, block(): pl.pallas_call(kernel, out_shape=(shape((BLK, DC), BF16), shape((BLK, DC)...  128 us

profile of v2, /device:TPU:0, one launch (start us, length us, event | category | flops | bytes accessed | tf_op | source)
XLA Modules:
  0.0 279.0 jit_solution(5231879396379560921)
XLA Ops:
  0.6 128.2 %shard_map.75 = (bf16[128,384]{1,0:T(8,128)(2,1)}, bf16[128,384]{1,0:T(8,128)(2,1)}, bf16[384,3072]{1,0:T(8,128)(2,1)}, bf16[3072,384]{1,0:T(8,128)(2,1)}) custom-call(bf16[128,384]{1,0:T(8,128)(2,1)} %tok_in.1, bf16[384,3072]{1,0:T(8,128)(2,1)} %wi_in.1, bf16[3072,384]{1,0:T(8,128)(2,1)} %wo_in.1, bf16[128,384]{1,0:T(8,128)(2,1)} %cot_in.1), custom_call_target="tpu_custom_call" | custom-call | flops 14499999744 | bytes 12000000 | tf_op jit(solution)/shard_map/pallas_call | solution.py:593
  128.9 150.1 %shard_map.76 = (bf16[128,384]{1,0:T(8,128)(2,1)}, bf16[128,384]{1,0:T(8,128)(2,1)}, bf16[384,3072]{1,0:T(8,128)(2,1)}, bf16[3072,384]{1,0:T(8,128)(2,1)}) custom-call(bf16[128,384]{1,0:T(8,128)(2,1)} %get-tuple-element.8.refs_0_, bf16[128,384]{1,0:T(8,128)(2,1)} %get-tuple-element.9.refs_1_, bf16[384,3072]{1,0:T(8,128)(2,1)} %get-tuple-element.10.refs_2_, ...), custom_call_target="tpu_custom_call" | custom-call | tf_op jit(solution)/shard_map/pallas_call | solution.py:579

commit v3 on v2

v3 whole, which is shorter than its diff:
```python
import functools

import jax
import jax.numpy as jnp
from jax import lax
from jax.experimental import pallas as pl
from jax.experimental.pallas import tpu as pltpu
from jax.sharding import PartitionSpec as P

F32 = jnp.float32
BF16 = jnp.bfloat16

TOK = 1024
BLK = 128
DC = 384
DP = 2 * DC
FH = 1536
FA = 896
FB = FH - FA

COPIES = 128
C_GELU = 0.7978845608028654
C_CUBE = 0.044715


def row_loop(rows, chunk, body):
    def step(i, carry):
        body(pl.multiple_of(i * chunk, chunk))
        return carry

    lax.fori_loop(0, rows // chunk, step, 0)


def tiles(count, body):
    def step(i, carry):
        body(i)
        return carry

    lax.fori_loop(0, count, step, 0)


class Links:
    def __init__(self, send, recv):
        self.send, self.recv, self.used = send, recv, 0
        self.started, self.taken = [], []
        row, col = lax.axis_index("row"), lax.axis_index("col")
        self.x, self.yh = row // 2, row % 2
        self.yl, self.z, self.k = col // 8, (col // 2) % 4, col % 2

    def device(self, **moved):
        at = {n: moved.get(n, getattr(self, n)) for n in ("x", "yh", "yl", "z", "k")}
        return (at["x"] * 2 + at["yh"], at["yl"] * 8 + at["z"] * 2 + at["k"])

    def ring(self, axis, step):
        return self.device(**{axis: lax.rem(getattr(self, axis) + step + 4, 4)})

    def other(self, axis):
        return self.device(**{axis: 1 - getattr(self, axis)})

    def copy(self, src, dst, device):
        i = self.used
        self.used += 1
        c = pltpu.make_async_remote_copy(
            src_ref=src,
            dst_ref=dst,
            send_sem=self.send.at[i],
            recv_sem=self.recv.at[i],
            device_id=device,
            device_id_type=pl.DeviceIdType.MESH,
        )
        c.start()
        self.started.append(c)
        return c

    def take(self, c):
        if all(c is not d for d in self.taken):
            c.wait_recv()
            self.taken.append(c)

    def place(self, axis, step):
        return lax.rem(getattr(self, axis) + step + 4, 4)


def rows_of(place, member, count=BLK, skip=0):
    return pl.ds(pl.multiple_of(place * (2 * BLK) + member * BLK + skip, 16), count)


class GatherRingLast:
    def __init__(self, links, ring, pair, buf, cols):
        self.l, self.ring, self.pair, self.buf, self.cols = links, ring, pair, buf, cols
        self.mine = getattr(links, pair)

    def at(self, step, member):
        return self.buf.at[rows_of(self.l.place(self.ring, step), member), self.cols]

    def send(self, ref, step):
        to = self.l.ring(self.ring, step) if step else self.l.other(self.pair)
        return self.l.copy(ref, ref, to)

    def start(self):
        own = self.at(0, self.mine)
        self.y = self.send(own, 0)
        self.own_p = self.send(own, 1)
        self.own_m = self.send(own, -1)

    def second(self):
        theirs = self.at(0, 1 - self.mine)
        self.oth_p = self.send(theirs, 1)
        self.oth_m = self.send(theirs, -1)

    def onward_p(self):
        self.far_p = self.send(self.at(-1, self.mine), 1)

    def onward_m(self):
        self.far_m = self.send(self.at(1, 1 - self.mine), -1)

    def arrived(self, step):
        if step == 0:
            return [self.y]
        if step == 2:
            return [self.far_p, self.far_m]
        return [self.own_p, self.oth_p] if step == -1 else [self.own_m, self.oth_m]

    def tasks(self, t, name, after):
        t.add(name + "0", after, lambda: [], self.start)
        t.add(name + "1", [name + "0"], lambda: [self.y], self.second)
        t.add(name + "p", [name + "0"], lambda: [self.own_p], self.onward_p)
        t.add(name + "m", [name + "1"], lambda: [self.oth_m], self.onward_m)


class GatherRingFirst:
    def __init__(self, links, ring, pair, buf, cols):
        self.l, self.ring, self.pair, self.buf, self.cols = links, ring, pair, buf, cols
        self.mine = getattr(links, pair)

    def at(self, step, count=BLK, skip=0):
        return self.buf.at[rows_of(self.l.place(self.ring, step), self.mine, count, skip), self.cols]

    def send(self, ref, step):
        to = self.l.ring(self.ring, step) if step else self.l.other(self.pair)
        return self.l.copy(ref, ref, to)

    def start(self):
        own = self.at(0)
        self.own_p = self.send(own, 1)
        self.own_m = self.send(own, -1)
        self.y0 = self.send(own, 0)

    def onward_p(self):
        self.far_p = self.send(self.at(-1, BLK // 2), 1)
        self.yp = self.send(self.at(-1), 0)

    def onward_m(self):
        self.far_m = self.send(self.at(1, BLK // 2, BLK // 2), -1)
        self.ym = self.send(self.at(1), 0)

    def across_p(self):
        self.yfp = self.send(self.at(2, BLK // 2), 0)

    def across_m(self):
        self.yfm = self.send(self.at(2, BLK // 2, BLK // 2), 0)

    def arrived(self, step):
        if step == 0:
            return [self.y0]
        if step == 2:
            return [self.yfp, self.yfm]
        return [self.yp] if step == -1 else [self.ym]

    def tasks(self, t, name, after):
        t.add(name + "0", after, lambda: [], self.start)
        t.add(name + "p", [name + "0"], lambda: [self.own_p], self.onward_p)
        t.add(name + "m", [name + "0"], lambda: [self.own_m], self.onward_m)
        t.add(name + "yp", [name + "p"], lambda: [self.far_p], self.across_p)
        t.add(name + "ym", [name + "m"], lambda: [self.far_m], self.across_m)


class ReduceRingFirst:
    def __init__(self, links, ring, pair, part, out, col, out_col, width, slots):
        self.l, self.ring, self.pair = links, ring, pair
        self.part, self.out, self.col, self.width, self.slots = part, out, col, width, slots
        self.out_cols = pl.ds(out_col, width)
        self.mine = getattr(links, pair)

    def block(self, step, member):
        return self.out.at[rows_of(self.l.place(self.ring, step), member), self.out_cols]

    def sent(self, step):
        l = self.l
        if step == 2:
            self.p2 = l.copy(self.block(2, 0), self.slots.at[0], l.ring(self.ring, 1))
            self.m2 = l.copy(self.block(2, 1), self.slots.at[1], l.ring(self.ring, -1))
        elif step == 1:
            self.p1 = l.copy(self.block(1, 1), self.slots.at[2], l.ring(self.ring, 1))
        elif step == -1:
            self.m1 = l.copy(self.block(-1, 0), self.slots.at[3], l.ring(self.ring, -1))

    def add(self, dst, start, *slots):
        def body(r):
            total = self.part[pl.ds(start + r, 32), pl.ds(self.col, self.width)]
            for s in slots:
                total = total + self.slots[s, pl.ds(r, 32), :].astype(F32)
            dst(r, total)

        row_loop(BLK, 32, body)

    def start_of(self, step, member):
        return pl.multiple_of(self.l.place(self.ring, step) * (2 * BLK) + member * BLK, BLK)

    def to_slot(self, slot):
        def put(r, total):
            self.slots[slot, pl.ds(r, 32), :] = total.astype(BF16)

        return put

    def combine_p(self):
        self.add(self.to_slot(7), self.start_of(1, 0), 0)
        self.pc = self.l.copy(self.slots.at[7], self.slots.at[4], self.l.ring(self.ring, 1))

    def combine_m(self):
        self.add(self.to_slot(8), self.start_of(-1, 1), 1)
        self.mc = self.l.copy(self.slots.at[8], self.slots.at[5], self.l.ring(self.ring, -1))

    def across(self):
        for member, slots in ((0, (4, 3)), (1, (2, 5))):
            start = self.start_of(0, member)

            def put(r, total, start=start):
                self.part[pl.ds(start + r, 32), pl.ds(self.col, self.width)] = total

            self.add(put, start, *slots)
        self.add(self.to_slot(9), self.start_of(0, 1 - self.mine))
        self.y = self.l.copy(self.slots.at[9], self.slots.at[6], self.l.other(self.pair))

    def tasks(self, t, name, put, after, first, last, final):
        t.add(name + "p", [after(1), first], lambda: [self.p2], self.combine_p)
        t.add(name + "m", [after(-1), first], lambda: [self.m2], self.combine_m)
        t.add(
            name + "y", [last, name + "p", name + "m"],
            lambda: [self.p1, self.m1, self.pc, self.mc], self.across,
        )
        t.add(
            name + "f", [name + "y"] + final, lambda: [self.y],
            lambda: self.add(put, self.start_of(0, self.mine), 6),
        )


class ReducePairFirst:
    def __init__(self, links, ring, pair, part, out, col, width, slots, halves):
        self.l, self.ring, self.pair = links, ring, pair
        self.part, self.out, self.col, self.width = part, out, col, width
        self.slots, self.halves = slots, halves
        self.mine = getattr(links, pair)
        self.y = {}

    def sent(self, step):
        rows = rows_of(self.l.place(self.ring, step), 1 - self.mine)
        block = self.out.at[rows, pl.ds(self.col, self.width)]
        self.y[step] = self.l.copy(block, self.slots.at[step % 4], self.l.other(self.pair))

    def add(self, dst, step, skip, count, *halves):
        start = pl.multiple_of(self.l.place(self.ring, step) * (2 * BLK) + self.mine * BLK + skip, 64)

        def body(r):
            total = self.part[pl.ds(start + r, 32), pl.ds(self.col, self.width)]
            total = total + self.slots[step % 4, pl.ds(skip + r, 32), :].astype(F32)
            for h in halves:
                total = total + self.halves[h, pl.ds(r, 32), :].astype(F32)
            dst(r, total)

        row_loop(count, 32, body)

    def to_half(self, half):
        def put(r, total):
            self.halves[half, pl.ds(r, 32), :] = total.astype(BF16)

        return put

    def ring_copy(self, src, dst, step):
        return self.l.copy(src, self.halves.at[dst], self.l.ring(self.ring, step))

    def far(self):
        def put(r, total):
            self.slots[4, pl.ds(r, 32), :] = total.astype(BF16)

        self.add(put, 2, 0, BLK)
        self.p2 = self.ring_copy(self.slots.at[4, pl.ds(0, BLK // 2)], 0, 1)
        self.m2 = self.ring_copy(self.slots.at[4, pl.ds(BLK // 2, BLK // 2)], 1, -1)

    def near_p(self):
        self.add(self.to_half(6), 1, BLK // 2, BLK // 2)
        self.p1 = self.ring_copy(self.halves.at[6], 2, 1)

    def near_m(self):
        self.add(self.to_half(7), -1, 0, BLK // 2)
        self.m1 = self.ring_copy(self.halves.at[7], 3, -1)

    def combine_p(self):
        self.add(self.to_half(8), 1, 0, BLK // 2, 0)
        self.pc = self.ring_copy(self.halves.at[8], 4, 1)

    def combine_m(self):
        self.add(self.to_half(9), -1, BLK // 2, BLK // 2, 1)
        self.mc = self.ring_copy(self.halves.at[9], 5, -1)

    def finish(self, put):
        half = BLK // 2
        self.add(put, 0, 0, half, 4, 3)
        self.add(lambda r, total: put(half + r, total), 0, half, half, 2, 5)

    def tasks(self, t, name, put, after, final):
        t.add(name + "2", [after(2)], lambda: [self.y[2]], self.far)
        t.add(name + "1", [after(1)], lambda: [self.y[1]], self.near_p)
        t.add(name + "3", [after(-1)], lambda: [self.y[-1]], self.near_m)
        t.add(name + "p", [name + "2", name + "1"], lambda: [self.p2], self.combine_p)
        t.add(name + "m", [name + "2", name + "3"], lambda: [self.m2], self.combine_m)
        t.add(
            name + "f", [after(0), name + "p", name + "m"] + final,
            lambda: [self.y[0], self.p1, self.m1, self.pc, self.mc],
            lambda: self.finish(put),
        )


class Tasks:
    def __init__(self, links):
        self.l, self.all = links, {}

    def add(self, name, after, waits, do):
        self.all[name] = (after, waits, do)

    def step(self, name):
        _, waits, do = self.all[name]
        for c in waits():
            self.l.take(c)
        do()


ORDER = (
    "t0", "t1", "tp", "ts0", "tm", "ts1", "ts-1", "c0", "ts2", "hpart2", "hpart1", "hpart-1", "hpart0", "c1",
    "cp", "cs0", "cm", "cs1", "cs-1", "ham", "cs2", "hap", "hb2", "gpart2", "gpart1", "gpart-1", "hb1",
    "gpart0", "hb3", "hbp", "hbm", "hbf", "hB0", "gb2", "hay", "gb1", "gb3", "gam", "gap", "gbp", "gbm",
    "haf", "hA0", "hBp", "hBm", "gbf", "gB0", "hA1", "ox0", "om0", "hByp", "hBym", "gay", "hAp", "gBp", "gBm",
    "hAm", "ox1", "gBym", "ox-1", "gByp", "om1", "om-1", "ox2", "go0", "go1", "om2", "or", "go2", "go3",
    "go4", "go5", "gaf", "gA0", "go", "odp", "odm", "ody", "gAp", "gA1", "ix0", "odf", "o", "im0", "gAm",
    "ix1", "im1", "ix-1", "ix2", "im-1", "gi0", "im2", "ir", "gi1", "gi", "gj0", "gj1", "gj", "idp", "idm",
    "idy", "idf", "i",
)


def run_tasks(t):
    done = set()
    for name in ORDER:
        assert done.issuperset(t.all[name][0]), name
        t.step(name)
        done.add(name)
    assert len(done) == len(t.all)


def dot(a, b, left, right):
    return lax.dot_general(a, b, (((left,), (right,)), ((), ())), preferred_element_type=F32)


STEPS = (2, 1, -1, 0)


def kernel(
    tok_in, wi_in, wo_in, cot_in,
    out_ref, gt_ref, gi_ref, go_ref,
    tok, cot, wi, wo,
    part_h, part_g, send_h, send_g,
    ra_h, ra_g, rb_h, rb_g, rh_h, rh_g,
    hid, acts, ghid,
    sib_in, rbuf, rd,
    gi, go, final,
    send, recv, local,
):
    l = Links(send, recv)
    t = Tasks(l)
    k = l.k
    sib = l.other("k")

    barrier = pltpu.get_barrier_semaphore()
    near = [sib, l.other("yl"), l.other("yh")]
    near += [l.ring(a, s) for a in ("z", "x") for s in (1, -1)]
    for d in near:
        pl.semaphore_signal(barrier, inc=1, device_id=d, device_id_type=pl.DeviceIdType.MESH)

    my_d = pl.ds(pl.multiple_of(k * DC, 128), DC)
    its_d = pl.ds(pl.multiple_of((1 - k) * DC, 128), DC)
    my_f = pl.ds(pl.multiple_of(k * FH, 128), FH)
    its_f = pl.ds(pl.multiple_of((1 - k) * FH, 128), FH)
    own_rows = rows_of(l.x, l.yh)

    load_tok = pltpu.make_async_copy(tok_in, tok.at[own_rows, my_d], local.at[0])
    load_cot = pltpu.make_async_copy(cot_in, cot.at[own_rows, my_d], local.at[1])
    load_wi = pltpu.make_async_copy(wi_in.at[:, my_f], wi.at[my_d], local.at[2])
    load_wo = pltpu.make_async_copy(wo_in.at[my_f], wo.at[:, my_d], local.at[3])
    for c in (load_tok, load_wi, load_cot, load_wo):
        c.start()
    pl.semaphore_wait(barrier, len(near))

    def pair_rows(axis, step):
        return pl.ds(pl.multiple_of(l.place(axis, step) * (2 * BLK), 2 * BLK), 2 * BLK)

    shared = {}

    def gather_tokens(name, buf, load, weight, target, after):
        g = GatherRingLast(l, "x", "yh", buf, my_d)

        def start():
            load.wait()
            g.start()
            shared[name + "w"] = l.copy(weight, target, sib)

        g.tasks(t, name, after)
        t.add(name + "0", after, lambda: [], start)

        def share(step):
            def do():
                ref = buf.at[pair_rows("x", step), my_d]
                shared[name + str(step)] = l.copy(ref, ref, sib)

            return do

        for step, before in ((0, ["1"]), (1, ["1"]), (-1, ["1"]), (2, ["p", "m"])):
            t.add(
                name + "s" + str(step), [name + b for b in before],
                lambda step=step: g.arrived(step), share(step),
            )

    gather_tokens("t", tok, load_tok, wi_in.at[:, its_f], wi.at[my_d], [])
    gather_tokens("c", cot, load_cot, wo_in.at[its_f], wo.at[:, my_d], ["ts1", "ts-1"])

    def put_hidden(col, width):
        cols = pl.ds(col, width)

        def put(r, h):
            hid[pl.ds(r, 32), cols] = h
            tanh = jnp.tanh(C_GELU * (h + C_CUBE * (h * h * h)))
            acts[pl.ds(own + r, 32), cols] = (0.5 * h * (1.0 + tanh)).astype(BF16)

        return put

    def put_grad(col, width):
        cols = pl.ds(col, width)

        def put(r, total):
            h = hid[pl.ds(r, 32), cols]
            square = h * h
            tanh = jnp.tanh(C_GELU * (h + C_CUBE * (square * h)))
            slope = 0.5 * (1.0 + tanh)
            slope += (0.5 * C_GELU) * h * (1.0 - tanh * tanh) * (1.0 + 3.0 * C_CUBE * square)
            ghid[pl.ds(own + r, 32), cols] = (total * slope).astype(BF16)

        return put

    own = pl.multiple_of(l.z * (2 * BLK) + l.yl * BLK, BLK)

    def reduction(name, source, load, product, part, out, slots_a, slots_b, halves, put, gathered, final):
        ring = ReduceRingFirst(l, "z", "yl", part, out, 0, 0, FA, slots_a)
        pair = ReducePairFirst(l, "z", "yl", part, out, FA, FB, slots_b, halves)

        def partial(step):
            def do():
                if step == STEPS[0]:
                    load.wait()
                rows = pair_rows("z", step)

                def tile(n):
                    cols = pl.ds(pl.multiple_of(n * 512, 512), 512)
                    total = product(rows, cols)
                    part[rows, cols] = total
                    out[rows, cols] = total.astype(BF16)

                tiles(FH // 512, tile)
                pair.sent(step)
                ring.sent(step)

            return do

        def part_of(step):
            return name + "part" + str(step)

        shares = [source + "s" + str(s) for s in STEPS]
        for i, step in enumerate(STEPS):
            t.add(
                part_of(step), shares if i == 0 else [part_of(STEPS[i - 1])],
                lambda: [shared[source + "w"]] + [shared[source + str(s)] for s in STEPS], partial(step),
            )
        ring.tasks(t, name + "a", put(0, FA), part_of, part_of(2), part_of(0), [f + "af" for f in final])
        pair.tasks(t, name + "b", put(FA, FB), part_of, [f + "bf" for f in final])
        a = GatherRingLast(l, "z", "yl", gathered, pl.ds(0, FA))
        b = GatherRingFirst(l, "z", "yl", gathered, pl.ds(FA, FB))
        a.tasks(t, name + "A", [name + "af"])
        b.tasks(t, name + "B", [name + "bf"])
        return a, b

    gathers_h = reduction(
        "h", "t", load_wi, lambda rows, cols: dot(tok[rows, :], wi[:, cols], 1, 0),
        part_h, send_h, ra_h, rb_h, rh_h, put_hidden, acts, [],
    )
    gathers_g = reduction(
        "g", "c", load_wo, lambda rows, cols: dot(cot[rows, :], wo[cols, :], 1, 1),
        part_g, send_g, ra_g, rb_g, rh_g, put_grad, ghid, ["h"],
    )

    merged = {}

    def projection(name, which, before, gathers, part, lhs, weight, right, target):
        final_sum = ReduceRingFirst(l, "x", "yh", part, rbuf.at[which], DP, 0, DC, rd.at[which])

        def project(step):
            def do():
                rows = pair_rows("z", step)
                part[rows, pl.ds(0, DP)] = dot(lhs[rows, :], weight[...], 1, right)
                merged[name + str(step)] = l.copy(part.at[rows, its_d], sib_in.at[which, rows], sib)

            return do

        def merge(step):
            def do():
                start = pl.multiple_of(l.place("z", step) * (2 * BLK), 2 * BLK)

                def body(r):
                    at = pl.ds(start + r, 32)
                    total = part[at, my_d] + sib_in[which, at, :]
                    part[at, pl.ds(DP, DC)] = total
                    rbuf[which, at, :] = total.astype(BF16)

                row_loop(2 * BLK, 32, body)

            return do

        for step, need in ((0, ["A1", "B0"]), (1, ["A1", "Bm"]), (-1, ["A1", "Bp"]), (2, ["Ap", "Am", "Byp", "Bym"])):
            t.add(
                name + "x" + str(step), [before + n for n in need] + [before + "af", before + "bf"],
                lambda step=step: gathers[0].arrived(step) + gathers[1].arrived(step), project(step),
            )
            t.add(
                name + "m" + str(step), [name + "x" + str(step)],
                lambda step=step: [merged[name + str(step)]], merge(step),
            )

        def go_round():
            for step in STEPS:
                final_sum.sent(step)

        merges = [name + "m" + str(s) for s in STEPS]
        t.add(name + "r", merges, lambda: [], go_round)

        def put(r, total):
            final[which, pl.ds(r, 32), :] = total.astype(BF16)

        final_sum.tasks(t, name + "d", put, lambda s: name + "r", name + "r", name + "r", [])
        return pltpu.make_async_copy(final.at[which], target, local.at[4 + which])

    out_done = projection("o", 0, "h", gathers_h, part_h, acts, wo, 0, out_ref)
    gt_done = projection("i", 1, "g", gathers_g, part_g, ghid, wi, 1, gt_ref)
    t.add("o", ["odf"], lambda: [], out_done.start)
    t.add("i", ["idf"], lambda: [], gt_done.start)

    whole_h = ["ox" + str(s) for s in STEPS] + ["cs" + str(s) for s in STEPS]
    whole_g = ["ix" + str(s) for s in STEPS]
    go_tile = 256

    def grad_out_tile(m):
        def do():
            cols = pl.ds(m * go_tile, go_tile)
            go[cols, :] = dot(acts[:, cols], cot[...], 0, 0).astype(BF16)

        return do

    go_tiles = ["go" + str(m) for m in range(FH // go_tile)]
    for m, name in enumerate(go_tiles):
        t.add(name, whole_h + ["gpart2"], lambda: [], grad_out_tile(m))
    go_done = pltpu.make_async_copy(go.at[:, my_d], go_ref.at[my_f], local.at[6])
    gi_done = pltpu.make_async_copy(gi.at[my_d], gi_ref.at[:, my_f], local.at[7])
    ends = []

    def send_go():
        go_done.start()
        ends.append(l.copy(go.at[:, its_d], go_ref.at[my_f], sib))

    t.add("go", go_tiles, lambda: [], send_go)

    def grad_in_tile(which, n):
        def do():
            cols = pl.ds(n * DP, DP)
            gi[which, cols] = dot(tok[:, which], ghid[:, cols], 0, 0).astype(BF16)

        return do

    for n in range(2):
        t.add("gi" + str(n), whole_g, lambda: [], grad_in_tile(its_d, n))
        t.add("gj" + str(n), whole_g, lambda: [], grad_in_tile(my_d, n))
    t.add("gi", ["gi0", "gi1"], lambda: [], lambda: ends.append(l.copy(gi.at[its_d], gi_ref.at[:, my_f], sib)))
    t.add("gj", ["gj0", "gj1"], lambda: [], gi_done.start)

    run_tasks(t)

    for c in ends:
        l.take(c)
    for c in (go_done, gi_done, out_done, gt_done):
        c.wait()
    for c in l.started:
        c.wait_send()


def hand_over(*refs):
    results, targets, held, (arrive, leave) = refs[:4], refs[4:8], refs[8:12], refs[12:]
    ins, outs = [], []
    for src, dst, mid in zip(results, targets, held):
        parts = 4 if src.shape[0] > BLK else 1
        rows = src.shape[0] // parts
        for p in range(parts):
            at, i = pl.ds(p * rows, rows), len(ins)
            ins.append(pltpu.make_async_copy(src.at[at], mid.at[at], arrive.at[i]))
            outs.append(pltpu.make_async_copy(mid.at[at], dst.at[at], leave.at[i]))
    for c in ins:
        c.start()
    for c, d in zip(ins, outs):
        c.wait()
        d.start()
    for d in outs:
        d.wait()


def local(tokens, weight_in, weight_out, cotangent):
    results = block(tokens, weight_in, weight_out, cotangent)
    any_space = pl.BlockSpec(memory_space=pl.ANY)
    return pl.pallas_call(
        hand_over,
        out_shape=tuple(jax.ShapeDtypeStruct(r.shape, r.dtype) for r in results),
        in_specs=[any_space] * 4,
        out_specs=(any_space,) * 4,
        scratch_shapes=[pltpu.VMEM(r.shape, r.dtype) for r in results] + [pltpu.SemaphoreType.DMA((10,))] * 2,
        compiler_params=pltpu.CompilerParams(vmem_limit_bytes=60 * 1024 * 1024),
    )(*results)


def block(tokens, weight_in, weight_out, cotangent):
    any_space = pl.BlockSpec(memory_space=pl.ANY)
    shape = jax.ShapeDtypeStruct
    vmem = pltpu.VMEM
    return pl.pallas_call(
        kernel,
        out_shape=(
            shape((BLK, DC), BF16),
            shape((BLK, DC), BF16),
            shape((DC, 2 * FH), BF16),
            shape((2 * FH, DC), BF16),
        ),
        in_specs=[any_space] * 4,
        out_specs=(any_space,) * 4,
        scratch_shapes=[
            vmem((TOK, DP), BF16), vmem((TOK, DP), BF16), vmem((DP, FH), BF16), vmem((FH, DP), BF16),
            vmem((TOK, FH), F32), vmem((TOK, FH), F32), vmem((TOK, FH), BF16), vmem((TOK, FH), BF16),
            vmem((10, BLK, FA), BF16), vmem((10, BLK, FA), BF16),
            vmem((5, BLK, FB), BF16), vmem((5, BLK, FB), BF16),
            vmem((10, BLK // 2, FB), BF16), vmem((10, BLK // 2, FB), BF16),
            vmem((BLK, FH), F32), vmem((TOK, FH), BF16), vmem((TOK, FH), BF16),
            vmem((2, TOK, DC), F32), vmem((2, TOK, DC), BF16),
            vmem((2, 10, BLK, DC), BF16),
            vmem((DP, FH), BF16), vmem((FH, DP), BF16), vmem((2, BLK, DC), BF16),
            pltpu.SemaphoreType.DMA((COPIES,)), pltpu.SemaphoreType.DMA((COPIES,)),
            pltpu.SemaphoreType.DMA((8,)),
        ],
        compiler_params=pltpu.CompilerParams(
            collective_id=0, has_side_effects=True, vmem_limit_bytes=60 * 1024 * 1024
        ),
        cost_estimate=pl.CostEstimate(flops=14_500_000_000, bytes_accessed=12_000_000, transcendentals=400_000),
    )(tokens, weight_in, weight_out, cotangent)


def solution(mesh):
    placed = (P("row", "col"), P("col", "row"), P("row", "col"), P("row", "col"))
    return jax.shard_map(
        local,
        mesh=mesh,
        in_specs=placed,
        out_specs=(P("row", "col"), P("row", "col"), P("col", "row"), P("row", "col")),
        check_vma=False,
    )
```

time: 279 us -> 145 us (0.52)
  Pallas kernels: 278 us -> 143 us
    pallas_call x1, Pallas kernels: 150 us -> 4.47 us  [local(): pl.pallas_call(hand_over, out_shape=tuple((jax.ShapeDtypeStruct(r.shape,...]
    pallas_call x1, Pallas kernels: 128 us -> 139 us  [block(): pl.pallas_call(kernel, out_shape=(shape((BLK, DC), BF16), shape((BLK, DC)...]
where the time goes in v3:
time: 145 us; the launch traced here: 144 us
  Pallas kernels  143 us (99%)
    pallas_call x1, Pallas kernels, block(): pl.pallas_call(kernel, out_shape=(shape((BLK, DC), BF16), shape((BLK, DC)...  139 us
    pallas_call x1, Pallas kernels, local(): pl.pallas_call(hand_over, out_shape=tuple((jax.ShapeDtypeStruct(r.shape,...  4.47 us

profile of v3, /device:TPU:0, one launch (start us, length us, event | category | flops | bytes accessed | tf_op | source)
XLA Modules:
  0.0 144.2 jit_solution(9407214106635502519)
XLA Ops:
  0.6 138.9 %shard_map.75 = (bf16[128,384]{1,0:T(8,128)(2,1)}, bf16[128,384]{1,0:T(8,128)(2,1)}, bf16[384,3072]{1,0:T(8,128)(2,1)}, bf16[3072,384]{1,0:T(8,128)(2,1)}) custom-call(bf16[128,384]{1,0:T(8,128)(2,1)} %tok_in.1, bf16[384,3072]{1,0:T(8,128)(2,1)} %wi_in.1, bf16[3072,384]{1,0:T(8,128)(2,1)} %wo_in.1, bf16[128,384]{1,0:T(8,128)(2,1)} %cot_in.1), custom_call_target="tpu_custom_call" | custom-call | flops 14499999744 | bytes 12000000 | tf_op jit(solution)/shard_map/pallas_call | solution.py:645
  139.6 4.5 %shard_map.76 = (bf16[128,384]{1,0:T(8,128)(2,1)}, bf16[128,384]{1,0:T(8,128)(2,1)}, bf16[384,3072]{1,0:T(8,128)(2,1)}, bf16[3072,384]{1,0:T(8,128)(2,1)}) custom-call(bf16[128,384]{1,0:T(8,128)(2,1)} %get-tuple-element.8.refs_0_, bf16[128,384]{1,0:T(8,128)(2,1)} %get-tuple-element.9.refs_1_, bf16[384,3072]{1,0:T(8,128)(2,1)} %get-tuple-element.10.refs_2_, ...), custom_call_target="tpu_custom_call" | custom-call | tf_op jit(solution)/shard_map/pallas_call | solution.py:631

commit v4 on v3

--- a/solution.py
+++ b/solution.py
@@ -19,6 +19,7 @@
 FB = FH - FA
 
 COPIES = 128
+ROWS = 16
 C_GELU = 0.7978845608028654
 C_CUBE = 0.044715
 
@@ -197,19 +198,19 @@
 
     def add(self, dst, start, *slots):
         def body(r):
-            total = self.part[pl.ds(start + r, 32), pl.ds(self.col, self.width)]
+            total = self.part[pl.ds(start + r, ROWS), pl.ds(self.col, self.width)]
             for s in slots:
-                total = total + self.slots[s, pl.ds(r, 32), :].astype(F32)
+                total = total + self.slots[s, pl.ds(r, ROWS), :].astype(F32)
             dst(r, total)
 
-        row_loop(BLK, 32, body)
+        row_loop(BLK, ROWS, body)
 
     def start_of(self, step, member):
         return pl.multiple_of(self.l.place(self.ring, step) * (2 * BLK) + member * BLK, BLK)
 
     def to_slot(self, slot):
         def put(r, total):
-            self.slots[slot, pl.ds(r, 32), :] = total.astype(BF16)
+            self.slots[slot, pl.ds(r, ROWS), :] = total.astype(BF16)
 
         return put
 
@@ -226,7 +227,7 @@
             start = self.start_of(0, member)
 
             def put(r, total, start=start):
-                self.part[pl.ds(start + r, 32), pl.ds(self.col, self.width)] = total
+                self.part[pl.ds(start + r, ROWS), pl.ds(self.col, self.width)] = total
 
             self.add(put, start, *slots)
         self.add(self.to_slot(9), self.start_of(0, 1 - self.mine))
@@ -262,17 +263,17 @@
         start = pl.multiple_of(self.l.place(self.ring, step) * (2 * BLK) + self.mine * BLK + skip, 64)
 
         def body(r):
-            total = self.part[pl.ds(start + r, 32), pl.ds(self.col, self.width)]
-            total = total + self.slots[step % 4, pl.ds(skip + r, 32), :].astype(F32)
+            total = self.part[pl.ds(start + r, ROWS), pl.ds(self.col, self.width)]
+            total = total + self.slots[step % 4, pl.ds(skip + r, ROWS), :].astype(F32)
             for h in halves:
-                total = total + self.halves[h, pl.ds(r, 32), :].astype(F32)
+                total = total + self.halves[h, pl.ds(r, ROWS), :].astype(F32)
             dst(r, total)
 
-        row_loop(count, 32, body)
+        row_loop(count, ROWS, body)
 
     def to_half(self, half):
         def put(r, total):
-            self.halves[half, pl.ds(r, 32), :] = total.astype(BF16)
+            self.halves[half, pl.ds(r, ROWS), :] = total.astype(BF16)
 
         return put
 
@@ -281,7 +282,7 @@
 
     def far(self):
         def put(r, total):
-            self.slots[4, pl.ds(r, 32), :] = total.astype(BF16)
+            self.slots[4, pl.ds(r, ROWS), :] = total.astype(BF16)
 
         self.add(put, 2, 0, BLK)
         self.p2 = self.ring_copy(self.slots.at[4, pl.ds(0, BLK // 2)], 0, 1)
@@ -337,13 +338,12 @@
 
 ORDER = (
     "t0", "t1", "tp", "ts0", "tm", "ts1", "ts-1", "c0", "ts2", "hpart2", "hpart1", "hpart-1", "hpart0", "c1",
-    "cp", "cs0", "cm", "cs1", "cs-1", "ham", "cs2", "hap", "hb2", "gpart2", "gpart1", "gpart-1", "hb1",
-    "gpart0", "hb3", "hbp", "hbm", "hbf", "hB0", "gb2", "hay", "gb1", "gb3", "gam", "gap", "gbp", "gbm",
-    "haf", "hA0", "hBp", "hBm", "gbf", "gB0", "hA1", "ox0", "om0", "hByp", "hBym", "gay", "hAp", "gBp", "gBm",
-    "hAm", "ox1", "gBym", "ox-1", "gByp", "om1", "om-1", "ox2", "go0", "go1", "om2", "or", "go2", "go3",
-    "go4", "go5", "gaf", "gA0", "go", "odp", "odm", "ody", "gAp", "gA1", "ix0", "odf", "o", "im0", "gAm",
-    "ix1", "im1", "ix-1", "ix2", "im-1", "gi0", "im2", "ir", "gi1", "gi", "gj0", "gj1", "gj", "idp", "idm",
-    "idy", "idf", "i",
+    "cp", "cs0", "turn", "cm", "cs1", "cs-1", "ham", "cs2", "hap", "hb2", "gpart2", "gpart1", "gpart-1",
+    "hb1", "gpart0", "hb3", "hbp", "hbm", "hbf", "hB0", "gb2", "gb1", "hay", "gb3", "gam", "gap", "gbm",
+    "gbp", "haf", "hA0", "hBp", "hBm", "gbf", "gB0", "hA1", "ox0", "om0", "hByp", "hBym", "gay", "hAp", "gBm",
+    "gBp", "hAm", "ox1", "gBym", "ox-1", "gByp", "om1", "om-1", "ox2", "go0", "om2", "or", "go1", "gaf",
+    "gA0", "go", "odp", "odm", "ody", "gA1", "gAp", "ix0", "odf", "im0", "o", "gAm", "ix1", "im1", "ix-1",
+    "ix2", "gi0", "im-1", "im2", "ir", "gi", "gj0", "gj", "idp", "idm", "idy", "idf", "i",
 )
 
 
@@ -371,7 +371,7 @@
     ra_h, ra_g, rb_h, rb_g, rh_h, rh_g,
     hid, acts, ghid,
     sib_in, rbuf, rd,
-    gi, go, final,
+    gi, go, final, turned,
     send, recv, local,
 ):
     l = Links(send, recv)
@@ -435,9 +435,9 @@
         cols = pl.ds(col, width)
 
         def put(r, h):
-            hid[pl.ds(r, 32), cols] = h
+            hid[pl.ds(r, ROWS), cols] = h
             tanh = jnp.tanh(C_GELU * (h + C_CUBE * (h * h * h)))
-            acts[pl.ds(own + r, 32), cols] = (0.5 * h * (1.0 + tanh)).astype(BF16)
+            acts[pl.ds(own + r, ROWS), cols] = (0.5 * h * (1.0 + tanh)).astype(BF16)
 
         return put
 
@@ -445,12 +445,12 @@
         cols = pl.ds(col, width)
 
         def put(r, total):
-            h = hid[pl.ds(r, 32), cols]
+            h = hid[pl.ds(r, ROWS), cols]
             square = h * h
             tanh = jnp.tanh(C_GELU * (h + C_CUBE * (square * h)))
             slope = 0.5 * (1.0 + tanh)
             slope += (0.5 * C_GELU) * h * (1.0 - tanh * tanh) * (1.0 + 3.0 * C_CUBE * square)
-            ghid[pl.ds(own + r, 32), cols] = (total * slope).astype(BF16)
+            ghid[pl.ds(own + r, ROWS), cols] = (total * slope).astype(BF16)
 
         return put
 
@@ -467,12 +467,12 @@
                 rows = pair_rows("z", step)
 
                 def tile(n):
-                    cols = pl.ds(pl.multiple_of(n * 512, 512), 512)
+                    cols = pl.ds(pl.multiple_of(n * 256, 256), 256)
                     total = product(rows, cols)
                     part[rows, cols] = total
                     out[rows, cols] = total.astype(BF16)
 
-                tiles(FH // 512, tile)
+                tiles(FH // 256, tile)
                 pair.sent(step)
                 ring.sent(step)
 
@@ -512,7 +512,12 @@
         def project(step):
             def do():
                 rows = pair_rows("z", step)
-                part[rows, pl.ds(0, DP)] = dot(lhs[rows, :], weight[...], 1, right)
+
+                def tile(n):
+                    cols = pl.ds(pl.multiple_of(n * 256, 256), 256)
+                    part[rows, cols] = dot(lhs[rows, :], weight[(cols, slice(None))[::2 * right - 1]], 1, right)
+
+                tiles(DP // 256, tile)
                 merged[name + str(step)] = l.copy(part.at[rows, its_d], sib_in.at[which, rows], sib)
 
             return do
@@ -522,12 +527,12 @@
                 start = pl.multiple_of(l.place("z", step) * (2 * BLK), 2 * BLK)
 
                 def body(r):
-                    at = pl.ds(start + r, 32)
+                    at = pl.ds(start + r, ROWS)
                     total = part[at, my_d] + sib_in[which, at, :]
                     part[at, pl.ds(DP, DC)] = total
                     rbuf[which, at, :] = total.astype(BF16)
 
-                row_loop(2 * BLK, 32, body)
+                row_loop(2 * BLK, ROWS, body)
 
             return do
 
@@ -549,7 +554,7 @@
         t.add(name + "r", merges, lambda: [], go_round)
 
         def put(r, total):
-            final[which, pl.ds(r, 32), :] = total.astype(BF16)
+            final[which, pl.ds(r, ROWS), :] = total.astype(BF16)
 
         final_sum.tasks(t, name + "d", put, lambda s: name + "r", name + "r", name + "r", [])
         return pltpu.make_async_copy(final.at[which], target, local.at[4 + which])
@@ -561,18 +566,16 @@
 
     whole_h = ["ox" + str(s) for s in STEPS] + ["cs" + str(s) for s in STEPS]
     whole_g = ["ix" + str(s) for s in STEPS]
-    go_tile = 256
-
-    def grad_out_tile(m):
-        def do():
-            cols = pl.ds(m * go_tile, go_tile)
+
+    def grad_out_tiles(half):
+        def tile(n):
+            cols = pl.ds(pl.multiple_of(half * (FH // 2) + n * 256, 256), 256)
             go[cols, :] = dot(acts[:, cols], cot[...], 0, 0).astype(BF16)
 
-        return do
-
-    go_tiles = ["go" + str(m) for m in range(FH // go_tile)]
-    for m, name in enumerate(go_tiles):
-        t.add(name, whole_h + ["gpart2"], lambda: [], grad_out_tile(m))
+        return lambda: tiles(FH // 512, tile)
+
+    for half in range(2):
+        t.add("go" + str(half), whole_h + ["gpart2"], lambda: [], grad_out_tiles(half))
     go_done = pltpu.make_async_copy(go.at[:, my_d], go_ref.at[my_f], local.at[6])
     gi_done = pltpu.make_async_copy(gi.at[my_d], gi_ref.at[:, my_f], local.at[7])
     ends = []
@@ -581,20 +584,28 @@
         go_done.start()
         ends.append(l.copy(go.at[:, its_d], go_ref.at[my_f], sib))
 
-    t.add("go", go_tiles, lambda: [], send_go)
-
-    def grad_in_tile(which, n):
-        def do():
-            cols = pl.ds(n * DP, DP)
-            gi[which, cols] = dot(tok[:, which], ghid[:, cols], 0, 0).astype(BF16)
-
-        return do
-
-    for n in range(2):
-        t.add("gi" + str(n), whole_g, lambda: [], grad_in_tile(its_d, n))
-        t.add("gj" + str(n), whole_g, lambda: [], grad_in_tile(my_d, n))
-    t.add("gi", ["gi0", "gi1"], lambda: [], lambda: ends.append(l.copy(gi.at[its_d], gi_ref.at[:, my_f], sib)))
-    t.add("gj", ["gj0", "gj1"], lambda: [], gi_done.start)
+    t.add("go", ["go0", "go1"], lambda: [], send_go)
+
+    def turn_tokens():
+        def tile(n):
+            cols = pl.ds(pl.multiple_of(n * 128, 128), 128)
+            turned[cols, :] = tok[:, cols].T
+
+        tiles(DP // 128, tile)
+
+    t.add("turn", ["hpart0"], lambda: [], turn_tokens)
+
+    def grad_in_tiles(rows):
+        def tile(n):
+            cols = pl.ds(pl.multiple_of(n * 256, 256), 256)
+            gi[rows, cols] = dot(turned[rows, :], ghid[:, cols], 1, 0).astype(BF16)
+
+        return lambda: tiles(FH // 256, tile)
+
+    t.add("gi0", whole_g + ["turn"], lambda: [], grad_in_tiles(its_d))
+    t.add("gj0", whole_g + ["turn"], lambda: [], grad_in_tiles(my_d))
+    t.add("gi", ["gi0"], lambda: [], lambda: ends.append(l.copy(gi.at[its_d], gi_ref.at[:, my_f], sib)))
+    t.add("gj", ["gj0"], lambda: [], gi_done.start)
 
     run_tasks(t)
 
@@ -661,7 +672,7 @@
             vmem((BLK, FH), F32), vmem((TOK, FH), BF16), vmem((TOK, FH), BF16),
             vmem((2, TOK, DC), F32), vmem((2, TOK, DC), BF16),
             vmem((2, 10, BLK, DC), BF16),
-            vmem((DP, FH), BF16), vmem((FH, DP), BF16), vmem((2, BLK, DC), BF16),
+            vmem((DP, FH), BF16), vmem((FH, DP), BF16), vmem((2, BLK, DC), BF16), vmem((DP, TOK), BF16),
             pltpu.SemaphoreType.DMA((COPIES,)), pltpu.SemaphoreType.DMA((COPIES,)),
             pltpu.SemaphoreType.DMA((8,)),
         ],

time: 145 us -> 145 us (level)
  no operation moved by 1% of the time
where the time goes in v4:
time: 145 us
  Pallas kernels  144 us (99%)
    pallas_call x1, Pallas kernels, block(): pl.pallas_call(kernel, out_shape=(shape((BLK, DC), BF16), shape((BLK, DC)...  139 us
    pallas_call x1, Pallas kernels, local(): pl.pallas_call(hand_over, out_shape=tuple((jax.ShapeDtypeStruct(r.shape,...  4.47 us

profile of v4, /device:TPU:0, one launch (start us, length us, event | category | flops | bytes accessed | tf_op | source)
XLA Modules:
  0.0 144.6 jit_solution(13500204031134511445)
XLA Ops:
  0.6 139.5 %shard_map.75 = (bf16[128,384]{1,0:T(8,128)(2,1)}, bf16[128,384]{1,0:T(8,128)(2,1)}, bf16[384,3072]{1,0:T(8,128)(2,1)}, bf16[3072,384]{1,0:T(8,128)(2,1)}) custom-call(bf16[128,384]{1,0:T(8,128)(2,1)} %tok_in.1, bf16[384,3072]{1,0:T(8,128)(2,1)} %wi_in.1, bf16[3072,384]{1,0:T(8,128)(2,1)} %wo_in.1, bf16[128,384]{1,0:T(8,128)(2,1)} %cot_in.1), custom_call_target="tpu_custom_call" | custom-call | flops 14499999744 | bytes 12000000 | tf_op jit(solution)/shard_map/pallas_call | solution.py:656
  140.1 4.5 %shard_map.76 = (bf16[128,384]{1,0:T(8,128)(2,1)}, bf16[128,384]{1,0:T(8,128)(2,1)}, bf16[384,3072]{1,0:T(8,128)(2,1)}, bf16[3072,384]{1,0:T(8,128)(2,1)}) custom-call(bf16[128,384]{1,0:T(8,128)(2,1)} %get-tuple-element.8.refs_0_, bf16[128,384]{1,0:T(8,128)(2,1)} %get-tuple-element.9.refs_1_, bf16[384,3072]{1,0:T(8,128)(2,1)} %get-tuple-element.10.refs_2_, ...), custom_call_target="tpu_custom_call" | custom-call | tf_op jit(solution)/shard_map/pallas_call | solution.py:642

commit v5 on v4

--- a/solution.py
+++ b/solution.py
@@ -337,13 +337,12 @@
 
 
 ORDER = (
-    "t0", "t1", "tp", "ts0", "tm", "ts1", "ts-1", "c0", "ts2", "hpart2", "hpart1", "hpart-1", "hpart0", "c1",
-    "cp", "cs0", "turn", "cm", "cs1", "cs-1", "ham", "cs2", "hap", "hb2", "gpart2", "gpart1", "gpart-1",
-    "hb1", "gpart0", "hb3", "hbp", "hbm", "hbf", "hB0", "gb2", "gb1", "hay", "gb3", "gam", "gap", "gbm",
-    "gbp", "haf", "hA0", "hBp", "hBm", "gbf", "gB0", "hA1", "ox0", "om0", "hByp", "hBym", "gay", "hAp", "gBm",
-    "gBp", "hAm", "ox1", "gBym", "ox-1", "gByp", "om1", "om-1", "ox2", "go0", "om2", "or", "go1", "gaf",
-    "gA0", "go", "odp", "odm", "ody", "gA1", "gAp", "ix0", "odf", "im0", "o", "gAm", "ix1", "im1", "ix-1",
-    "ix2", "gi0", "im-1", "im2", "ir", "gi", "gj0", "gj", "idp", "idm", "idy", "idf", "i",
+    "cs", "ts", "t0", "tw", "t1", "tp", "c0", "c1", "tm", "cm", "cp", "hpart2", "cw", "hpart1", "hpart-1",
+    "hpart0", "ham", "hb2", "turn", "hap", "hb1", "hbp", "hb3", "hbm", "hbf", "hay", "hB0", "gpart2",
+    "gpart1", "gpart-1", "gpart0", "hBp", "hBm", "gam", "gap", "hByp", "hBym", "haf", "hA0", "gay", "gb2",
+    "hAp", "gb1", "gbp", "gb3", "gbm", "gbf", "gB0", "hA1", "ox0", "gaf", "gA0", "gBp", "gBm", "gByp", "gBym",
+    "hAm", "ox1", "gA1", "gAp", "ix0", "ox-1", "ox2", "gAm", "ix1", "ix-1", "or", "go0", "ix2", "ir", "gi0",
+    "odp", "odm", "gi1", "go1", "gj0", "idp", "idm", "ody", "gj1", "idy", "odf", "os", "idf", "is", "o", "i",
 )
 
 
@@ -370,7 +369,7 @@
     part_h, part_g, send_h, send_g,
     ra_h, ra_g, rb_h, rb_g, rh_h, rh_g,
     hid, acts, ghid,
-    sib_in, rbuf, rd,
+    summed, summed_in, rbuf, rd,
     gi, go, final, turned,
     send, recv, local,
 ):
@@ -402,34 +401,37 @@
     def pair_rows(axis, step):
         return pl.ds(pl.multiple_of(l.place(axis, step) * (2 * BLK), 2 * BLK), 2 * BLK)
 
+    def to_sibling(pairs):
+        return [l.copy(src, dst, sib) for src, dst in pairs]
+
     shared = {}
 
-    def gather_tokens(name, buf, load, weight, target, after):
-        g = GatherRingLast(l, "x", "yh", buf, my_d)
-
-        def start():
+    def gather_tokens(name, buf, load, weights, after, weights_after):
+        g = GatherRingLast(l, "x", "yh", buf, pl.ds(0, DP))
+
+        def share():
             load.wait()
-            g.start()
-            shared[name + "w"] = l.copy(weight, target, sib)
-
-        g.tasks(t, name, after)
-        t.add(name + "0", after, lambda: [], start)
-
-        def share(step):
-            def do():
-                ref = buf.at[pair_rows("x", step), my_d]
-                shared[name + str(step)] = l.copy(ref, ref, sib)
-
-            return do
-
-        for step, before in ((0, ["1"]), (1, ["1"]), (-1, ["1"]), (2, ["p", "m"])):
-            t.add(
-                name + "s" + str(step), [name + b for b in before],
-                lambda step=step: g.arrived(step), share(step),
-            )
-
-    gather_tokens("t", tok, load_tok, wi_in.at[:, its_f], wi.at[my_d], [])
-    gather_tokens("c", cot, load_cot, wo_in.at[its_f], wo.at[:, my_d], ["ts1", "ts-1"])
+            piece = buf.at[own_rows, my_d]
+            shared[name] = to_sibling([(piece, piece)])
+
+        def send_weights():
+            shared[name + "w"] = to_sibling(weights)
+
+        t.add(name + "s", [], lambda: [], share)
+        g.tasks(t, name, [name + "s"] + after)
+        t.add(name + "0", [name + "s"] + after, lambda: shared[name], g.start)
+        t.add(name + "w", weights_after, lambda: [], send_weights)
+        return g
+
+    def split(start, count, parts):
+        return [pl.ds(pl.multiple_of(start + i * (count // parts), 16), count // parts) for i in range(parts)]
+
+    rows_in = zip(split(0, DC, 4), split(k * DC, DC, 4))
+    wi_copies = [(wi_in.at[a, its_f], wi.at[b]) for a, b in rows_in]
+    rows_out = zip(split((1 - k) * FH, FH, 4), split(0, FH, 4))
+    wo_copies = [(wo_in.at[a], wo.at[b, my_d]) for a, b in rows_out]
+    gather_t = gather_tokens("t", tok, load_tok, wi_copies, [], ["t0"])
+    gather_c = gather_tokens("c", cot, load_cot, wo_copies, ["t1"], ["hpart2"])
 
     def put_hidden(col, width):
         cols = pl.ds(col, width)
@@ -456,7 +458,7 @@
 
     own = pl.multiple_of(l.z * (2 * BLK) + l.yl * BLK, BLK)
 
-    def reduction(name, source, load, product, part, out, slots_a, slots_b, halves, put, gathered, final):
+    def reduction(name, source, tokens_of, load, product, part, out, slots_a, slots_b, halves, put, gathered, final):
         ring = ReduceRingFirst(l, "z", "yl", part, out, 0, 0, FA, slots_a)
         pair = ReducePairFirst(l, "z", "yl", part, out, FA, FB, slots_b, halves)
 
@@ -481,11 +483,11 @@
         def part_of(step):
             return name + "part" + str(step)
 
-        shares = [source + "s" + str(s) for s in STEPS]
+        before = [source + s for s in ("s", "p", "m", "w")]
         for i, step in enumerate(STEPS):
             t.add(
-                part_of(step), shares if i == 0 else [part_of(STEPS[i - 1])],
-                lambda: [shared[source + "w"]] + [shared[source + str(s)] for s in STEPS], partial(step),
+                part_of(step), before if i == 0 else [part_of(STEPS[i - 1])],
+                lambda: shared[source + "w"] + [c for s in STEPS for c in tokens_of.arrived(s)], partial(step),
             )
         ring.tasks(t, name + "a", put(0, FA), part_of, part_of(2), part_of(0), [f + "af" for f in final])
         pair.tasks(t, name + "b", put(FA, FB), part_of, [f + "bf" for f in final])
@@ -496,18 +498,16 @@
         return a, b
 
     gathers_h = reduction(
-        "h", "t", load_wi, lambda rows, cols: dot(tok[rows, :], wi[:, cols], 1, 0),
+        "h", "t", gather_t, load_wi, lambda rows, cols: dot(tok[rows, :], wi[:, cols], 1, 0),
         part_h, send_h, ra_h, rb_h, rh_h, put_hidden, acts, [],
     )
     gathers_g = reduction(
-        "g", "c", load_wo, lambda rows, cols: dot(cot[rows, :], wo[cols, :], 1, 1),
+        "g", "c", gather_c, load_wo, lambda rows, cols: dot(cot[rows, :], wo[cols, :], 1, 1),
         part_g, send_g, ra_g, rb_g, rh_g, put_grad, ghid, ["h"],
     )
 
-    merged = {}
-
     def projection(name, which, before, gathers, part, lhs, weight, right, target):
-        final_sum = ReduceRingFirst(l, "x", "yh", part, rbuf.at[which], DP, 0, DC, rd.at[which])
+        final_sum = ReduceRingFirst(l, "x", "yh", part, rbuf.at[which], 0, 0, DP, rd.at[which])
 
         def project(step):
             def do():
@@ -515,24 +515,11 @@
 
                 def tile(n):
                     cols = pl.ds(pl.multiple_of(n * 256, 256), 256)
-                    part[rows, cols] = dot(lhs[rows, :], weight[(cols, slice(None))[::2 * right - 1]], 1, right)
+                    total = dot(lhs[rows, :], weight[(cols, slice(None))[:: 2 * right - 1]], 1, right)
+                    part[rows, cols] = total
+                    rbuf[which, rows, cols] = total.astype(BF16)
 
                 tiles(DP // 256, tile)
-                merged[name + str(step)] = l.copy(part.at[rows, its_d], sib_in.at[which, rows], sib)
-
-            return do
-
-        def merge(step):
-            def do():
-                start = pl.multiple_of(l.place("z", step) * (2 * BLK), 2 * BLK)
-
-                def body(r):
-                    at = pl.ds(start + r, ROWS)
-                    total = part[at, my_d] + sib_in[which, at, :]
-                    part[at, pl.ds(DP, DC)] = total
-                    rbuf[which, at, :] = total.astype(BF16)
-
-                row_loop(2 * BLK, ROWS, body)
 
             return do
 
@@ -541,50 +528,60 @@
                 name + "x" + str(step), [before + n for n in need] + [before + "af", before + "bf"],
                 lambda step=step: gathers[0].arrived(step) + gathers[1].arrived(step), project(step),
             )
-            t.add(
-                name + "m" + str(step), [name + "x" + str(step)],
-                lambda step=step: [merged[name + str(step)]], merge(step),
-            )
 
         def go_round():
             for step in STEPS:
                 final_sum.sent(step)
 
-        merges = [name + "m" + str(s) for s in STEPS]
-        t.add(name + "r", merges, lambda: [], go_round)
+        t.add(name + "r", [name + "x" + str(s) for s in STEPS], lambda: [], go_round)
 
         def put(r, total):
-            final[which, pl.ds(r, ROWS), :] = total.astype(BF16)
+            summed[which, pl.ds(r, ROWS), :] = total
 
         final_sum.tasks(t, name + "d", put, lambda s: name + "r", name + "r", name + "r", [])
-        return pltpu.make_async_copy(final.at[which], target, local.at[4 + which])
+        done = pltpu.make_async_copy(final.at[which], target, local.at[4 + which])
+
+        def exchange():
+            shared[name] = to_sibling([(summed.at[which, :, its_d], summed_in.at[which])])
+
+        def conclude():
+            def body(r):
+                at = pl.ds(r, ROWS)
+                final[which, at, :] = (summed[which, at, my_d] + summed_in[which, at, :]).astype(BF16)
+
+            row_loop(BLK, ROWS, body)
+            done.start()
+
+        t.add(name + "s", [name + "df"], lambda: [], exchange)
+        t.add(name, [name + "s"], lambda: shared[name], conclude)
+        return done
 
     out_done = projection("o", 0, "h", gathers_h, part_h, acts, wo, 0, out_ref)
     gt_done = projection("i", 1, "g", gathers_g, part_g, ghid, wi, 1, gt_ref)
-    t.add("o", ["odf"], lambda: [], out_done.start)
-    t.add("i", ["idf"], lambda: [], gt_done.start)
-
-    whole_h = ["ox" + str(s) for s in STEPS] + ["cs" + str(s) for s in STEPS]
+
+    whole_h = ["ox" + str(s) for s in STEPS]
     whole_g = ["ix" + str(s) for s in STEPS]
+
+    go_done = pltpu.make_async_copy(go.at[:, my_d], go_ref.at[my_f], local.at[6])
+    gi_done = pltpu.make_async_copy(gi.at[my_d], gi_ref.at[:, my_f], local.at[7])
+    ends = []
 
     def grad_out_tiles(half):
         def tile(n):
             cols = pl.ds(pl.multiple_of(half * (FH // 2) + n * 256, 256), 256)
             go[cols, :] = dot(acts[:, cols], cot[...], 0, 0).astype(BF16)
 
-        return lambda: tiles(FH // 512, tile)
-
-    for half in range(2):
-        t.add("go" + str(half), whole_h + ["gpart2"], lambda: [], grad_out_tiles(half))
-    go_done = pltpu.make_async_copy(go.at[:, my_d], go_ref.at[my_f], local.at[6])
-    gi_done = pltpu.make_async_copy(gi.at[my_d], gi_ref.at[:, my_f], local.at[7])
-    ends = []
-
-    def send_go():
-        go_done.start()
-        ends.append(l.copy(go.at[:, its_d], go_ref.at[my_f], sib))
-
-    t.add("go", ["go0", "go1"], lambda: [], send_go)
+        def do():
+            tiles(FH // 512, tile)
+            here, there = split(half * (FH // 2), FH // 2, 2), split(k * FH + half * (FH // 2), FH // 2, 2)
+            ends.extend(to_sibling([(go.at[a, its_d], go_ref.at[b]) for a, b in zip(here, there)]))
+            if half == 1:
+                go_done.start()
+
+        return do
+
+    t.add("go0", whole_h + ["gpart2"], lambda: [], grad_out_tiles(0))
+    t.add("go1", ["go0"], lambda: [], grad_out_tiles(1))
 
     def turn_tokens():
         def tile(n):
@@ -595,17 +592,29 @@
 
     t.add("turn", ["hpart0"], lambda: [], turn_tokens)
 
-    def grad_in_tiles(rows):
+    def grad_in_tiles(rows, half, last):
         def tile(n):
-            cols = pl.ds(pl.multiple_of(n * 256, 256), 256)
+            cols = pl.ds(pl.multiple_of(half * DP + n * 256, 256), 256)
             gi[rows, cols] = dot(turned[rows, :], ghid[:, cols], 1, 0).astype(BF16)
 
-        return lambda: tiles(FH // 256, tile)
-
-    t.add("gi0", whole_g + ["turn"], lambda: [], grad_in_tiles(its_d))
-    t.add("gj0", whole_g + ["turn"], lambda: [], grad_in_tiles(my_d))
-    t.add("gi", ["gi0"], lambda: [], lambda: ends.append(l.copy(gi.at[its_d], gi_ref.at[:, my_f], sib)))
-    t.add("gj", ["gj0"], lambda: [], gi_done.start)
+        def do():
+            tiles(DP // 256, tile)
+            last(half)
+
+        return do
+
+    def send_gi(half):
+        here, there = pl.ds(half * DP, DP), pl.ds(pl.multiple_of(k * FH + half * DP, 128), DP)
+        parts = zip(split((1 - k) * DC, DC, 2), split(0, DC, 2))
+        ends.extend(to_sibling([(gi.at[a, here], gi_ref.at[b, there]) for a, b in parts]))
+
+    def store_gi(half):
+        if half == 1:
+            gi_done.start()
+
+    for name, rows, last in (("gi", its_d, send_gi), ("gj", my_d, store_gi)):
+        t.add(name + "0", whole_g + ["turn"], lambda: [], grad_in_tiles(rows, 0, last))
+        t.add(name + "1", [name + "0"], lambda: [], grad_in_tiles(rows, 1, last))
 
     run_tasks(t)
 
@@ -670,8 +679,8 @@
             vmem((5, BLK, FB), BF16), vmem((5, BLK, FB), BF16),
             vmem((10, BLK // 2, FB), BF16), vmem((10, BLK // 2, FB), BF16),
             vmem((BLK, FH), F32), vmem((TOK, FH), BF16), vmem((TOK, FH), BF16),
-            vmem((2, TOK, DC), F32), vmem((2, TOK, DC), BF16),
-            vmem((2, 10, BLK, DC), BF16),
+            vmem((2, BLK, DP), F32), vmem((2, BLK, DC), F32), vmem((2, TOK, DP), BF16),
+            vmem((2, 10, BLK, DP), BF16),
             vmem((DP, FH), BF16), vmem((FH, DP), BF16), vmem((2, BLK, DC), BF16), vmem((DP, TOK), BF16),
             pltpu.SemaphoreType.DMA((COPIES,)), pltpu.SemaphoreType.DMA((COPIES,)),
             pltpu.SemaphoreType.DMA((8,)),

time: 145 us -> 165 us (1.14); the launches traced: 145 us -> 162 us
  Pallas kernels: 144 us -> 162 us
    pallas_call x1, Pallas kernels: 139 us -> 157 us  [block(): pl.pallas_call(kernel, out_shape=(shape((BLK, DC), BF16), shape((BLK, DC)...]
where the time goes in v5:
time: 165 us; the launch traced here: 162 us
  Pallas kernels  162 us (98%)
    pallas_call x1, Pallas kernels, block(): pl.pallas_call(kernel, out_shape=(shape((BLK, DC), BF16), shape((BLK, DC)...  157 us
    pallas_call x1, Pallas kernels, local(): pl.pallas_call(hand_over, out_shape=tuple((jax.ShapeDtypeStruct(r.shape,...  4.47 us

profile of v5, /device:TPU:0, one launch (start us, length us, event | category | flops | bytes accessed | tf_op | source)
XLA Modules:
  0.0 162.2 jit_solution(7800020186630256629)
XLA Ops:
  0.6 157.1 %shard_map.75 = (bf16[128,384]{1,0:T(8,128)(2,1)}, bf16[128,384]{1,0:T(8,128)(2,1)}, bf16[384,3072]{1,0:T(8,128)(2,1)}, bf16[3072,384]{1,0:T(8,128)(2,1)}) custom-call(bf16[128,384]{1,0:T(8,128)(2,1)} %tok_in.1, bf16[384,3072]{1,0:T(8,128)(2,1)} %wi_in.1, bf16[3072,384]{1,0:T(8,128)(2,1)} %wo_in.1, bf16[128,384]{1,0:T(8,128)(2,1)} %cot_in.1), custom_call_target="tpu_custom_call" | custom-call | flops 14499999744 | bytes 12000000 | tf_op jit(solution)/shard_map/pallas_call | solution.py:665
  157.8 4.5 %shard_map.76 = (bf16[128,384]{1,0:T(8,128)(2,1)}, bf16[128,384]{1,0:T(8,128)(2,1)}, bf16[384,3072]{1,0:T(8,128)(2,1)}, bf16[3072,384]{1,0:T(8,128)(2,1)}) custom-call(bf16[128,384]{1,0:T(8,128)(2,1)} %get-tuple-element.8.refs_0_, bf16[128,384]{1,0:T(8,128)(2,1)} %get-tuple-element.9.refs_1_, bf16[384,3072]{1,0:T(8,128)(2,1)} %get-tuple-element.10.refs_2_, ...), custom_call_target="tpu_custom_call" | custom-call | tf_op jit(solution)/shard_map/pallas_call | solution.py:651

commit v6 on v4

--- a/solution.py
+++ b/solution.py
@@ -87,22 +87,22 @@
 
 
 class GatherRingLast:
-    def __init__(self, links, ring, pair, buf, cols):
+    def __init__(self, links, ring, pair, buf, cols, source=None):
         self.l, self.ring, self.pair, self.buf, self.cols = links, ring, pair, buf, cols
-        self.mine = getattr(links, pair)
+        self.mine, self.source = getattr(links, pair), source
 
     def at(self, step, member):
         return self.buf.at[rows_of(self.l.place(self.ring, step), member), self.cols]
 
-    def send(self, ref, step):
+    def send(self, ref, step, source=None):
         to = self.l.ring(self.ring, step) if step else self.l.other(self.pair)
-        return self.l.copy(ref, ref, to)
+        return self.l.copy(ref if source is None else source, ref, to)
 
     def start(self):
         own = self.at(0, self.mine)
-        self.y = self.send(own, 0)
-        self.own_p = self.send(own, 1)
-        self.own_m = self.send(own, -1)
+        self.y = self.send(own, 0, self.source)
+        self.own_p = self.send(own, 1, self.source)
+        self.own_m = self.send(own, -1, self.source)
 
     def second(self):
         theirs = self.at(0, 1 - self.mine)
@@ -337,13 +337,13 @@
 
 
 ORDER = (
-    "t0", "t1", "tp", "ts0", "tm", "ts1", "ts-1", "c0", "ts2", "hpart2", "hpart1", "hpart-1", "hpart0", "c1",
-    "cp", "cs0", "turn", "cm", "cs1", "cs-1", "ham", "cs2", "hap", "hb2", "gpart2", "gpart1", "gpart-1",
-    "hb1", "gpart0", "hb3", "hbp", "hbm", "hbf", "hB0", "gb2", "gb1", "hay", "gb3", "gam", "gap", "gbm",
-    "gbp", "haf", "hA0", "hBp", "hBm", "gbf", "gB0", "hA1", "ox0", "om0", "hByp", "hBym", "gay", "hAp", "gBm",
-    "gBp", "hAm", "ox1", "gBym", "ox-1", "gByp", "om1", "om-1", "ox2", "go0", "om2", "or", "go1", "gaf",
-    "gA0", "go", "odp", "odm", "ody", "gA1", "gAp", "ix0", "odf", "im0", "o", "gAm", "ix1", "im1", "ix-1",
-    "ix2", "gi0", "im-1", "im2", "ir", "gi", "gj0", "gj", "idp", "idm", "idy", "idf", "i",
+    "t0", "t1", "ts0", "c0", "tp", "ts-1", "ts1", "tm", "ts2", "c1", "cp", "hpart2", "cm", "hpart1",
+    "hpart-1", "hpart0", "cs0", "cs-1", "cs2", "turn", "hb2", "hap", "ham", "cs1", "gpart2", "gpart1", "hb1",
+    "gpart-1", "gpart0", "hb3", "hbp", "hbm", "hay", "gb2", "gb1", "gam", "gb3", "gap", "hbf", "hB0", "gbp",
+    "gbm", "haf", "hA0", "gay", "hA1", "ox0", "hBm", "hBp", "gbf", "gB0", "gaf", "hAp", "ox-1", "ox1", "hAm",
+    "gA0", "hByp", "om-1", "om1", "hBym", "gBm", "gBp", "om0", "gA1", "ix0", "im0", "ox2", "go1", "om2", "or",
+    "gAp", "gBym", "go0", "gAm", "ix1", "odp", "odm", "gByp", "ix-1", "im1", "ody", "im-1", "ix2", "gi0",
+    "im2", "ir", "odf", "gi", "gj0", "gj", "idp", "o", "go", "idm", "idy", "idf", "i",
 )
 
 
@@ -404,11 +404,10 @@
 
     shared = {}
 
-    def gather_tokens(name, buf, load, weight, target, after):
-        g = GatherRingLast(l, "x", "yh", buf, my_d)
+    def gather_tokens(name, buf, source, load, weight, target, after):
+        g = GatherRingLast(l, "x", "yh", buf, my_d, source)
 
         def start():
-            load.wait()
             g.start()
             shared[name + "w"] = l.copy(weight, target, sib)
 
@@ -417,6 +416,8 @@
 
         def share(step):
             def do():
+                if step == 0:
+                    load.wait()
                 ref = buf.at[pair_rows("x", step), my_d]
                 shared[name + str(step)] = l.copy(ref, ref, sib)
 
@@ -428,8 +429,8 @@
                 lambda step=step: g.arrived(step), share(step),
             )
 
-    gather_tokens("t", tok, load_tok, wi_in.at[:, its_f], wi.at[my_d], [])
-    gather_tokens("c", cot, load_cot, wo_in.at[its_f], wo.at[:, my_d], ["ts1", "ts-1"])
+    gather_tokens("t", tok, tok_in, load_tok, wi_in.at[:, its_f], wi.at[my_d], [])
+    gather_tokens("c", cot, cot_in, load_cot, wo_in.at[its_f], wo.at[:, my_d], ["t1"])
 
     def put_hidden(col, width):
         cols = pl.ds(col, width)

time: 145 us -> 133 us (0.917)
  Pallas kernels: 144 us -> 132 us
    pallas_call x1, Pallas kernels: 139 us -> 128 us  [block(): pl.pallas_call(kernel, out_shape=(shape((BLK, DC), BF16), shape((BLK, DC)...]
where the time goes in v6:
time: 133 us
  Pallas kernels  132 us (99%)
    pallas_call x1, Pallas kernels, block(): pl.pallas_call(kernel, out_shape=(shape((BLK, DC), BF16), shape((BLK, DC)...  128 us
    pallas_call x1, Pallas kernels, local(): pl.pallas_call(hand_over, out_shape=tuple((jax.ShapeDtypeStruct(r.shape,...  4.47 us

profile of v6, /device:TPU:0, one launch (start us, length us, event | category | flops | bytes accessed | tf_op | source)
XLA Modules:
  0.0 132.9 jit_solution(7832357383037302590)
XLA Ops:
  0.6 127.7 %shard_map.75 = (bf16[128,384]{1,0:T(8,128)(2,1)}, bf16[128,384]{1,0:T(8,128)(2,1)}, bf16[384,3072]{1,0:T(8,128)(2,1)}, bf16[3072,384]{1,0:T(8,128)(2,1)}) custom-call(bf16[128,384]{1,0:T(8,128)(2,1)} %tok_in.1, bf16[384,3072]{1,0:T(8,128)(2,1)} %wi_in.1, bf16[3072,384]{1,0:T(8,128)(2,1)} %wo_in.1, bf16[128,384]{1,0:T(8,128)(2,1)} %cot_in.1), custom_call_target="tpu_custom_call" | custom-call | flops 14499999744 | bytes 12000000 | tf_op jit(solution)/shard_map/pallas_call | solution.py:657
  128.4 4.5 %shard_map.76 = (bf16[128,384]{1,0:T(8,128)(2,1)}, bf16[128,384]{1,0:T(8,128)(2,1)}, bf16[384,3072]{1,0:T(8,128)(2,1)}, bf16[3072,384]{1,0:T(8,128)(2,1)}) custom-call(bf16[128,384]{1,0:T(8,128)(2,1)} %get-tuple-element.8.refs_0_, bf16[128,384]{1,0:T(8,128)(2,1)} %get-tuple-element.9.refs_1_, bf16[384,3072]{1,0:T(8,128)(2,1)} %get-tuple-element.10.refs_2_, ...), custom_call_target="tpu_custom_call" | custom-call | tf_op jit(solution)/shard_map/pallas_call | solution.py:643

commit v7 on v6

--- a/solution.py
+++ b/solution.py
@@ -15,7 +15,7 @@
 DC = 384
 DP = 2 * DC
 FH = 1536
-FA = 896
+FA = 768
 FB = FH - FA
 
 COPIES = 128
@@ -59,8 +59,13 @@
         return self.device(**{axis: 1 - getattr(self, axis)})
 
     def copy(self, src, dst, device):
-        i = self.used
-        self.used += 1
+        c = self.plan(src, dst, device)
+        c.start()
+        return c
+
+    def plan(self, src, dst, device, slot=None):
+        i = self.used if slot is None else slot
+        self.used += slot is None
         c = pltpu.make_async_remote_copy(
             src_ref=src,
             dst_ref=dst,
@@ -69,8 +74,8 @@
             device_id=device,
             device_id_type=pl.DeviceIdType.MESH,
         )
-        c.start()
-        self.started.append(c)
+        if slot is None:
+            self.started.append(c)
         return c
 
     def take(self, c):
@@ -186,15 +191,32 @@
     def block(self, step, member):
         return self.out.at[rows_of(self.l.place(self.ring, step), member), self.out_cols]
 
-    def sent(self, step):
+    def plan(self):
         l = self.l
-        if step == 2:
-            self.p2 = l.copy(self.block(2, 0), self.slots.at[0], l.ring(self.ring, 1))
-            self.m2 = l.copy(self.block(2, 1), self.slots.at[1], l.ring(self.ring, -1))
-        elif step == 1:
-            self.p1 = l.copy(self.block(1, 1), self.slots.at[2], l.ring(self.ring, 1))
-        elif step == -1:
-            self.m1 = l.copy(self.block(-1, 0), self.slots.at[3], l.ring(self.ring, -1))
+        self.p2 = l.plan(self.block(2, 0), self.slots.at[0], l.ring(self.ring, 1))
+        self.m2 = l.plan(self.block(2, 1), self.slots.at[1], l.ring(self.ring, -1))
+        self.p1 = l.plan(self.block(1, 1), self.slots.at[2], l.ring(self.ring, 1))
+        self.m1 = l.plan(self.block(-1, 0), self.slots.at[3], l.ring(self.ring, -1))
+
+    def sent(self):
+        for c in (self.p2, self.m2, self.p1, self.m1):
+            c.start()
+
+    def sent_pair(self, place):
+        step = lax.rem(place - getattr(self.l, self.ring) + 4, 4)
+
+        @pl.when(step == 2)
+        def _():
+            self.p2.start()
+            self.m2.start()
+
+        @pl.when(step == 1)
+        def _():
+            self.p1.start()
+
+        @pl.when(step == 3)
+        def _():
+            self.m1.start()
 
     def add(self, dst, start, *slots):
         def body(r):
@@ -233,11 +255,11 @@
         self.add(self.to_slot(9), self.start_of(0, 1 - self.mine))
         self.y = self.l.copy(self.slots.at[9], self.slots.at[6], self.l.other(self.pair))
 
-    def tasks(self, t, name, put, after, first, last, final):
-        t.add(name + "p", [after(1), first], lambda: [self.p2], self.combine_p)
-        t.add(name + "m", [after(-1), first], lambda: [self.m2], self.combine_m)
+    def tasks(self, t, name, put, after, final):
+        t.add(name + "p", [after], lambda: [self.p2], self.combine_p)
+        t.add(name + "m", [after], lambda: [self.m2], self.combine_m)
         t.add(
-            name + "y", [last, name + "p", name + "m"],
+            name + "y", [after, name + "p", name + "m"],
             lambda: [self.p1, self.m1, self.pc, self.mc], self.across,
         )
         t.add(
@@ -252,19 +274,29 @@
         self.part, self.out, self.col, self.width = part, out, col, width
         self.slots, self.halves = slots, halves
         self.mine = getattr(links, pair)
-        self.y = {}
-
-    def sent(self, step):
-        rows = rows_of(self.l.place(self.ring, step), 1 - self.mine)
-        block = self.out.at[rows, pl.ds(self.col, self.width)]
-        self.y[step] = self.l.copy(block, self.slots.at[step % 4], self.l.other(self.pair))
+
+    def plan(self):
+        self.y = [self.to_pair(self.l.place("x", i), i) for i in range(4)]
+        self.first = self.l.used - 4
+
+    def to_pair(self, place, i, slot=None):
+        block = self.out.at[rows_of(place, 1 - self.mine), pl.ds(self.col, self.width)]
+        return self.l.plan(block, self.slots.at[i], self.l.other(self.pair), slot)
+
+    def from_x(self, step):
+        return lax.rem(self.l.place(self.ring, step) - self.l.x + 4, 4)
+
+    def came(self, step):
+        i = self.from_x(step)
+        return [self.to_pair(self.l.place(self.ring, step), i, self.first + i)]
 
     def add(self, dst, step, skip, count, *halves):
         start = pl.multiple_of(self.l.place(self.ring, step) * (2 * BLK) + self.mine * BLK + skip, 64)
+        slot = self.from_x(step)
 
         def body(r):
             total = self.part[pl.ds(start + r, ROWS), pl.ds(self.col, self.width)]
-            total = total + self.slots[step % 4, pl.ds(skip + r, ROWS), :].astype(F32)
+            total = total + self.slots[slot, pl.ds(skip + r, ROWS), :].astype(F32)
             for h in halves:
                 total = total + self.halves[h, pl.ds(r, ROWS), :].astype(F32)
             dst(r, total)
@@ -310,14 +342,14 @@
         self.add(lambda r, total: put(half + r, total), 0, half, half, 2, 5)
 
     def tasks(self, t, name, put, after, final):
-        t.add(name + "2", [after(2)], lambda: [self.y[2]], self.far)
-        t.add(name + "1", [after(1)], lambda: [self.y[1]], self.near_p)
-        t.add(name + "3", [after(-1)], lambda: [self.y[-1]], self.near_m)
+        t.add(name + "2", [after], lambda: self.came(2), self.far)
+        t.add(name + "1", [after], lambda: self.came(1), self.near_p)
+        t.add(name + "3", [after], lambda: self.came(-1), self.near_m)
         t.add(name + "p", [name + "2", name + "1"], lambda: [self.p2], self.combine_p)
         t.add(name + "m", [name + "2", name + "3"], lambda: [self.m2], self.combine_m)
         t.add(
-            name + "f", [after(0), name + "p", name + "m"] + final,
-            lambda: [self.y[0], self.p1, self.m1, self.pc, self.mc],
+            name + "f", [after, name + "p", name + "m"] + final,
+            lambda: self.came(0) + [self.p1, self.m1, self.pc, self.mc],
             lambda: self.finish(put),
         )
 
@@ -337,13 +369,13 @@
 
 
 ORDER = (
-    "t0", "t1", "ts0", "c0", "tp", "ts-1", "ts1", "tm", "ts2", "c1", "cp", "hpart2", "cm", "hpart1",
-    "hpart-1", "hpart0", "cs0", "cs-1", "cs2", "turn", "hb2", "hap", "ham", "cs1", "gpart2", "gpart1", "hb1",
-    "gpart-1", "gpart0", "hb3", "hbp", "hbm", "hay", "gb2", "gb1", "gam", "gb3", "gap", "hbf", "hB0", "gbp",
-    "gbm", "haf", "hA0", "gay", "hA1", "ox0", "hBm", "hBp", "gbf", "gB0", "gaf", "hAp", "ox-1", "ox1", "hAm",
-    "gA0", "hByp", "om-1", "om1", "hBym", "gBm", "gBp", "om0", "gA1", "ix0", "im0", "ox2", "go1", "om2", "or",
-    "gAp", "gBym", "go0", "gAm", "ix1", "odp", "odm", "gByp", "ix-1", "im1", "ody", "im-1", "ix2", "gi0",
-    "im2", "ir", "odf", "gi", "gj0", "gj", "idp", "o", "go", "idm", "idy", "idf", "i",
+    "t0", "tp", "t1", "ts0", "c0", "hpart0", "ts1", "tm", "ts-1", "cp", "c1", "cs0", "hpart1", "ts2",
+    "hpart-1", "cs1", "hpart2", "cs-1", "cm", "turn", "gpart0", "gpart1", "cs2", "gpart-1", "hb1", "gpart2",
+    "hap", "hb3", "ham", "hb2", "gam", "gap", "gb1", "hay", "hbp", "gb3", "hbm", "gb2", "gay", "haf", "hA0",
+    "hbf", "hB0", "gbp", "gaf", "gbm", "hBm", "gA0", "hAp", "hA1", "hBp", "ox0", "gbf", "gB0", "gA1", "hAm",
+    "hBym", "ox1", "ox-1", "hByp", "gBm", "ix0", "om0", "om-1", "gBp", "im0", "om1", "gAp", "gAm", "ox2",
+    "ix1", "gBym", "go0", "om2", "or", "gByp", "ix-1", "go1", "odp", "im-1", "odm", "ix2", "im1", "im2", "ir",
+    "ody", "go", "gj0", "gj", "idp", "idm", "odf", "gi0", "o", "gi", "idy", "idf", "i",
 )
 
 
@@ -361,6 +393,7 @@
 
 
 STEPS = (2, 1, -1, 0)
+ARRIVAL = (0, 1, -1, 2)
 
 
 def kernel(
@@ -463,9 +496,11 @@
 
         def partial(step):
             def do():
-                if step == STEPS[0]:
+                if step == ARRIVAL[0]:
                     load.wait()
-                rows = pair_rows("z", step)
+                    ring.plan()
+                    pair.plan()
+                rows = pair_rows("x", step)
 
                 def tile(n):
                     cols = pl.ds(pl.multiple_of(n * 256, 256), 256)
@@ -474,22 +509,20 @@
                     out[rows, cols] = total.astype(BF16)
 
                 tiles(FH // 256, tile)
-                pair.sent(step)
-                ring.sent(step)
+                pair.y[step % 4].start()
+                ring.sent_pair(l.place("x", step))
 
             return do
 
-        def part_of(step):
-            return name + "part" + str(step)
-
-        shares = [source + "s" + str(s) for s in STEPS]
-        for i, step in enumerate(STEPS):
+        for i, step in enumerate(ARRIVAL):
+            before = [source + "s" + str(step)] + [name + "part" + str(ARRIVAL[i - 1])] * (i > 0)
             t.add(
-                part_of(step), shares if i == 0 else [part_of(STEPS[i - 1])],
-                lambda: [shared[source + "w"]] + [shared[source + str(s)] for s in STEPS], partial(step),
+                name + "part" + str(step), before,
+                lambda step=step: [shared[source + "w"], shared[source + str(step)]], partial(step),
             )
-        ring.tasks(t, name + "a", put(0, FA), part_of, part_of(2), part_of(0), [f + "af" for f in final])
-        pair.tasks(t, name + "b", put(FA, FB), part_of, [f + "bf" for f in final])
+        last = name + "part" + str(ARRIVAL[-1])
+        ring.tasks(t, name + "a", put(0, FA), last, [f + "af" for f in final])
+        pair.tasks(t, name + "b", put(FA, FB), last, [f + "bf" for f in final])
         a = GatherRingLast(l, "z", "yl", gathered, pl.ds(0, FA))
         b = GatherRingFirst(l, "z", "yl", gathered, pl.ds(FA, FB))
         a.tasks(t, name + "A", [name + "af"])
@@ -548,8 +581,8 @@
             )
 
         def go_round():
-            for step in STEPS:
-                final_sum.sent(step)
+            final_sum.plan()
+            final_sum.sent()
 
         merges = [name + "m" + str(s) for s in STEPS]
         t.add(name + "r", merges, lambda: [], go_round)
@@ -557,7 +590,7 @@
         def put(r, total):
             final[which, pl.ds(r, ROWS), :] = total.astype(BF16)
 
-        final_sum.tasks(t, name + "d", put, lambda s: name + "r", name + "r", name + "r", [])
+        final_sum.tasks(t, name + "d", put, name + "r", [])
         return pltpu.make_async_copy(final.at[which], target, local.at[4 + which])
 
     out_done = projection("o", 0, "h", gathers_h, part_h, acts, wo, 0, out_ref)
@@ -594,7 +627,7 @@
 
         tiles(DP // 128, tile)
 
-    t.add("turn", ["hpart0"], lambda: [], turn_tokens)
+    t.add("turn", ["hpart2"], lambda: [], turn_tokens)
 
     def grad_in_tiles(rows):
         def tile(n):

time: 133 us -> 128 us (0.962)
  Pallas kernels: 132 us -> 127 us
    pallas_call x1, Pallas kernels: 128 us -> 123 us  [block(): pl.pallas_call(kernel, out_shape=(shape((BLK, DC), BF16), shape((BLK, DC)...]
where the time goes in v7:
time: 128 us
  Pallas kernels  127 us (99%)
    pallas_call x1, Pallas kernels, block(): pl.pallas_call(kernel, out_shape=(shape((BLK, DC), BF16), shape((BLK, DC)...  123 us
    pallas_call x1, Pallas kernels, local(): pl.pallas_call(hand_over, out_shape=tuple((jax.ShapeDtypeStruct(r.shape,...  4.47 us

profile of v7, /device:TPU:0, one launch (start us, length us, event | category | flops | bytes accessed | tf_op | source)
XLA Modules:
  0.0 127.9 jit_solution(6995056171876053737)
XLA Ops:
  0.6 122.8 %shard_map.75 = (bf16[128,384]{1,0:T(8,128)(2,1)}, bf16[128,384]{1,0:T(8,128)(2,1)}, bf16[384,3072]{1,0:T(8,128)(2,1)}, bf16[3072,384]{1,0:T(8,128)(2,1)}) custom-call(bf16[128,384]{1,0:T(8,128)(2,1)} %tok_in.1, bf16[384,3072]{1,0:T(8,128)(2,1)} %wi_in.1, bf16[3072,384]{1,0:T(8,128)(2,1)} %wo_in.1, bf16[128,384]{1,0:T(8,128)(2,1)} %cot_in.1), custom_call_target="tpu_custom_call" | custom-call | flops 14499999744 | bytes 12000000 | tf_op jit(solution)/shard_map/pallas_call | solution.py:690
  123.4 4.5 %shard_map.76 = (bf16[128,384]{1,0:T(8,128)(2,1)}, bf16[128,384]{1,0:T(8,128)(2,1)}, bf16[384,3072]{1,0:T(8,128)(2,1)}, bf16[3072,384]{1,0:T(8,128)(2,1)}) custom-call(bf16[128,384]{1,0:T(8,128)(2,1)} %get-tuple-element.8.refs_0_, bf16[128,384]{1,0:T(8,128)(2,1)} %get-tuple-element.9.refs_1_, bf16[384,3072]{1,0:T(8,128)(2,1)} %get-tuple-element.10.refs_2_, ...), custom_call_target="tpu_custom_call" | custom-call | tf_op jit(solution)/shard_map/pallas_call | solution.py:676

commit v8 on v7

--- a/solution.py
+++ b/solution.py
@@ -15,8 +15,9 @@
 DC = 384
 DP = 2 * DC
 FH = 1536
-FA = 768
-FB = FH - FA
+FA_H = 768
+FA_G = 896
+FA_D = 256
 
 COPIES = 128
 ROWS = 16
@@ -269,9 +270,10 @@
 
 
 class ReducePairFirst:
-    def __init__(self, links, ring, pair, part, out, col, width, slots, halves):
+    def __init__(self, links, ring, pair, part, out, col, out_col, width, slots, halves):
         self.l, self.ring, self.pair = links, ring, pair
         self.part, self.out, self.col, self.width = part, out, col, width
+        self.out_cols = pl.ds(out_col, width)
         self.slots, self.halves = slots, halves
         self.mine = getattr(links, pair)
 
@@ -280,7 +282,7 @@
         self.first = self.l.used - 4
 
     def to_pair(self, place, i, slot=None):
-        block = self.out.at[rows_of(place, 1 - self.mine), pl.ds(self.col, self.width)]
+        block = self.out.at[rows_of(place, 1 - self.mine), self.out_cols]
         return self.l.plan(block, self.slots.at[i], self.l.other(self.pair), slot)
 
     def from_x(self, step):
@@ -369,13 +371,13 @@
 
 
 ORDER = (
-    "t0", "tp", "t1", "ts0", "c0", "hpart0", "ts1", "tm", "ts-1", "cp", "c1", "cs0", "hpart1", "ts2",
-    "hpart-1", "cs1", "hpart2", "cs-1", "cm", "turn", "gpart0", "gpart1", "cs2", "gpart-1", "hb1", "gpart2",
-    "hap", "hb3", "ham", "hb2", "gam", "gap", "gb1", "hay", "hbp", "gb3", "hbm", "gb2", "gay", "haf", "hA0",
-    "hbf", "hB0", "gbp", "gaf", "gbm", "hBm", "gA0", "hAp", "hA1", "hBp", "ox0", "gbf", "gB0", "gA1", "hAm",
-    "hBym", "ox1", "ox-1", "hByp", "gBm", "ix0", "om0", "om-1", "gBp", "im0", "om1", "gAp", "gAm", "ox2",
-    "ix1", "gBym", "go0", "om2", "or", "gByp", "ix-1", "go1", "odp", "im-1", "odm", "ix2", "im1", "im2", "ir",
-    "ody", "go", "gj0", "gj", "idp", "idm", "odf", "gi0", "o", "gi", "idy", "idf", "i",
+    "t0", "tp", "t1", "ts0", "c0", "ts1", "hpart0", "tm", "ts-1", "c1", "cs0", "hpart1", "ts2", "hpart-1",
+    "cm", "cs1", "cp", "hpart2", "cs-1", "gpart0", "gpart1", "cs2", "gpart-1", "turn", "gpart2", "hap", "ham",
+    "gam", "hb1", "hb2", "gap", "hay", "hb3", "hbm", "hbp", "gay", "gb3", "gb2", "gb1", "haf", "hbf", "hA0",
+    "hB0", "gaf", "gA0", "hBm", "gbp", "gbm", "hBp", "hA1", "gbf", "gB0", "hAm", "hByp", "ox0", "hAp", "ox1",
+    "hBym", "ox-1", "gA1", "ix0", "gBm", "om0", "om1", "gBp", "om-1", "ox2", "gAp", "go0", "gAm", "ix1",
+    "om2", "or", "gByp", "im0", "gBym", "ix-1", "go1", "odm", "im-1", "ix2", "im1", "odp", "gj0", "im2", "ir",
+    "ie1", "ie2", "ie3", "go", "ody", "idm", "idp", "gi0", "gi", "idy", "odf", "iem", "iep", "ief", "idf",
 )
 
 
@@ -403,8 +405,8 @@
     part_h, part_g, send_h, send_g,
     ra_h, ra_g, rb_h, rb_g, rh_h, rh_g,
     hid, acts, ghid,
-    sib_in, rbuf, rd,
-    gi, go, final, turned,
+    sib_in, rbuf, rd_h, rd_g, re_g, rf_g,
+    gi, go, turned,
     send, recv, local,
 ):
     l = Links(send, recv)
@@ -490,9 +492,9 @@
 
     own = pl.multiple_of(l.z * (2 * BLK) + l.yl * BLK, BLK)
 
-    def reduction(name, source, load, product, part, out, slots_a, slots_b, halves, put, gathered, final):
-        ring = ReduceRingFirst(l, "z", "yl", part, out, 0, 0, FA, slots_a)
-        pair = ReducePairFirst(l, "z", "yl", part, out, FA, FB, slots_b, halves)
+    def reduction(name, fa, source, load, product, part, out, slots_a, slots_b, halves, put, gathered, final):
+        ring = ReduceRingFirst(l, "z", "yl", part, out, 0, 0, fa, slots_a)
+        pair = ReducePairFirst(l, "z", "yl", part, out, fa, fa, FH - fa, slots_b, halves)
 
         def partial(step):
             def do():
@@ -521,27 +523,31 @@
                 lambda step=step: [shared[source + "w"], shared[source + str(step)]], partial(step),
             )
         last = name + "part" + str(ARRIVAL[-1])
-        ring.tasks(t, name + "a", put(0, FA), last, [f + "af" for f in final])
-        pair.tasks(t, name + "b", put(FA, FB), last, [f + "bf" for f in final])
-        a = GatherRingLast(l, "z", "yl", gathered, pl.ds(0, FA))
-        b = GatherRingFirst(l, "z", "yl", gathered, pl.ds(FA, FB))
+        ring.tasks(t, name + "a", put(0, fa), last, final)
+        pair.tasks(t, name + "b", put(fa, FH - fa), last, final)
+        a = GatherRingLast(l, "z", "yl", gathered, pl.ds(0, fa))
+        b = GatherRingFirst(l, "z", "yl", gathered, pl.ds(fa, FH - fa))
         a.tasks(t, name + "A", [name + "af"])
         b.tasks(t, name + "B", [name + "bf"])
         return a, b
 
     gathers_h = reduction(
-        "h", "t", load_wi, lambda rows, cols: dot(tok[rows, :], wi[:, cols], 1, 0),
+        "h", FA_H, "t", load_wi, lambda rows, cols: dot(tok[rows, :], wi[:, cols], 1, 0),
         part_h, send_h, ra_h, rb_h, rh_h, put_hidden, acts, [],
     )
     gathers_g = reduction(
-        "g", "c", load_wo, lambda rows, cols: dot(cot[rows, :], wo[cols, :], 1, 1),
-        part_g, send_g, ra_g, rb_g, rh_g, put_grad, ghid, ["h"],
+        "g", FA_G, "c", load_wo, lambda rows, cols: dot(cot[rows, :], wo[cols, :], 1, 1),
+        part_g, send_g, ra_g, rb_g, rh_g, put_grad, ghid, ["haf", "hbf"],
     )
 
     merged = {}
 
-    def projection(name, which, before, gathers, part, lhs, weight, right, target):
-        final_sum = ReduceRingFirst(l, "x", "yh", part, rbuf.at[which], DP, 0, DC, rd.at[which])
+    def projection(name, which, before, gathers, part, lhs, weight, right, target, slots, split_slots):
+        wide = FA_D if split_slots else DC
+        ring = ReduceRingFirst(l, "x", "yh", part, rbuf.at[which], DP, 0, wide, slots)
+        pair = split_slots and ReducePairFirst(
+            l, "x", "yh", part, rbuf.at[which], DP + wide, wide, DC - wide, *split_slots
+        )
 
         def project(step):
             def do():
@@ -581,22 +587,28 @@
             )
 
         def go_round():
-            final_sum.plan()
-            final_sum.sent()
+            ring.plan()
+            ring.sent()
+            if pair:
+                pair.plan()
+                for i in (2, 1, 3, 0):
+                    pair.y[i].start()
 
         merges = [name + "m" + str(s) for s in STEPS]
         t.add(name + "r", merges, lambda: [], go_round)
 
-        def put(r, total):
-            final[which, pl.ds(r, ROWS), :] = total.astype(BF16)
-
-        final_sum.tasks(t, name + "d", put, name + "r", [])
-        return pltpu.make_async_copy(final.at[which], target, local.at[4 + which])
-
-    out_done = projection("o", 0, "h", gathers_h, part_h, acts, wo, 0, out_ref)
-    gt_done = projection("i", 1, "g", gathers_g, part_g, ghid, wi, 1, gt_ref)
-    t.add("o", ["odf"], lambda: [], out_done.start)
-    t.add("i", ["idf"], lambda: [], gt_done.start)
+        def put(col, width):
+            def body(r, total):
+                target[pl.ds(r, ROWS), pl.ds(col, width)] = total.astype(BF16)
+
+            return body
+
+        ring.tasks(t, name + "d", put(0, wide), name + "r", [])
+        if pair:
+            pair.tasks(t, name + "e", put(wide, DC - wide), name + "r", [])
+
+    projection("o", 0, "h", gathers_h, part_h, acts, wo, 0, out_ref, rd_h, ())
+    projection("i", 1, "g", gathers_g, part_g, ghid, wi, 1, gt_ref, rd_g, (re_g, rf_g))
 
     whole_h = ["ox" + str(s) for s in STEPS] + ["cs" + str(s) for s in STEPS]
     whole_g = ["ix" + str(s) for s in STEPS]
@@ -610,13 +622,16 @@
 
     for half in range(2):
         t.add("go" + str(half), whole_h + ["gpart2"], lambda: [], grad_out_tiles(half))
-    go_done = pltpu.make_async_copy(go.at[:, my_d], go_ref.at[my_f], local.at[6])
-    gi_done = pltpu.make_async_copy(gi.at[my_d], gi_ref.at[:, my_f], local.at[7])
     ends = []
 
     def send_go():
-        go_done.start()
         ends.append(l.copy(go.at[:, its_d], go_ref.at[my_f], sib))
+        own_start = pl.multiple_of(k * FH, 128)
+
+        def keep(r):
+            go_ref[pl.ds(own_start + r, 32), :] = go[pl.ds(r, 32), my_d]
+
+        row_loop(FH, 32, keep)
 
     t.add("go", ["go0", "go1"], lambda: [], send_go)
 
@@ -629,45 +644,39 @@
 
     t.add("turn", ["hpart2"], lambda: [], turn_tokens)
 
-    def grad_in_tiles(rows):
+    def grad_in_tiles(rows, start, target):
         def tile(n):
             cols = pl.ds(pl.multiple_of(n * 256, 256), 256)
-            gi[rows, cols] = dot(turned[rows, :], ghid[:, cols], 1, 0).astype(BF16)
+            at = pl.ds(pl.multiple_of(start + n * 256, 128), 256)
+            target[:, at] = dot(turned[rows, :], ghid[:, cols], 1, 0).astype(BF16)
 
         return lambda: tiles(FH // 256, tile)
 
-    t.add("gi0", whole_g + ["turn"], lambda: [], grad_in_tiles(its_d))
-    t.add("gj0", whole_g + ["turn"], lambda: [], grad_in_tiles(my_d))
-    t.add("gi", ["gi0"], lambda: [], lambda: ends.append(l.copy(gi.at[its_d], gi_ref.at[:, my_f], sib)))
-    t.add("gj", ["gj0"], lambda: [], gi_done.start)
+    t.add("gi0", whole_g + ["turn"], lambda: [], grad_in_tiles(its_d, 0, gi))
+    t.add("gj0", whole_g + ["turn"], lambda: [], grad_in_tiles(my_d, k * FH, gi_ref))
+    t.add("gi", ["gi0"], lambda: [], lambda: ends.append(l.copy(gi, gi_ref.at[:, my_f], sib)))
 
     run_tasks(t)
 
     for c in ends:
         l.take(c)
-    for c in (go_done, gi_done, out_done, gt_done):
-        c.wait()
     for c in l.started:
         c.wait_send()
 
 
 def hand_over(*refs):
-    results, targets, held, (arrive, leave) = refs[:4], refs[4:8], refs[8:12], refs[12:]
-    ins, outs = [], []
-    for src, dst, mid in zip(results, targets, held):
+    sems = refs[-1]
+    copies = []
+    for src, dst in zip(refs[:4], refs[4:8]):
         parts = 4 if src.shape[0] > BLK else 1
         rows = src.shape[0] // parts
         for p in range(parts):
-            at, i = pl.ds(p * rows, rows), len(ins)
-            ins.append(pltpu.make_async_copy(src.at[at], mid.at[at], arrive.at[i]))
-            outs.append(pltpu.make_async_copy(mid.at[at], dst.at[at], leave.at[i]))
-    for c in ins:
+            at = pl.ds(p * rows, rows)
+            copies.append(pltpu.make_async_copy(src.at[at], dst.at[at], sems.at[len(copies)]))
+    for c in copies:
         c.start()
-    for c, d in zip(ins, outs):
+    for c in copies:
         c.wait()
-        d.start()
-    for d in outs:
-        d.wait()
 
 
 def local(tokens, weight_in, weight_out, cotangent):
@@ -676,10 +685,9 @@
     return pl.pallas_call(
         hand_over,
         out_shape=tuple(jax.ShapeDtypeStruct(r.shape, r.dtype) for r in results),
-        in_specs=[any_space] * 4,
+        in_specs=[pl.BlockSpec(memory_space=pltpu.VMEM)] * 4,
         out_specs=(any_space,) * 4,
-        scratch_shapes=[pltpu.VMEM(r.shape, r.dtype) for r in results] + [pltpu.SemaphoreType.DMA((10,))] * 2,
-        compiler_params=pltpu.CompilerParams(vmem_limit_bytes=60 * 1024 * 1024),
+        scratch_shapes=[pltpu.SemaphoreType.DMA((10,))],
     )(*results)
 
 
@@ -690,28 +698,29 @@
     return pl.pallas_call(
         kernel,
         out_shape=(
-            shape((BLK, DC), BF16),
-            shape((BLK, DC), BF16),
-            shape((DC, 2 * FH), BF16),
-            shape((2 * FH, DC), BF16),
+            vmem((BLK, DC), BF16),
+            vmem((BLK, DC), BF16),
+            vmem((DC, 2 * FH), BF16),
+            vmem((2 * FH, DC), BF16),
         ),
         in_specs=[any_space] * 4,
-        out_specs=(any_space,) * 4,
+        out_specs=(pl.BlockSpec(memory_space=pltpu.VMEM),) * 4,
         scratch_shapes=[
             vmem((TOK, DP), BF16), vmem((TOK, DP), BF16), vmem((DP, FH), BF16), vmem((FH, DP), BF16),
             vmem((TOK, FH), F32), vmem((TOK, FH), F32), vmem((TOK, FH), BF16), vmem((TOK, FH), BF16),
-            vmem((10, BLK, FA), BF16), vmem((10, BLK, FA), BF16),
-            vmem((5, BLK, FB), BF16), vmem((5, BLK, FB), BF16),
-            vmem((10, BLK // 2, FB), BF16), vmem((10, BLK // 2, FB), BF16),
+            vmem((10, BLK, FA_H), BF16), vmem((10, BLK, FA_G), BF16),
+            vmem((5, BLK, FH - FA_H), BF16), vmem((5, BLK, FH - FA_G), BF16),
+            vmem((10, BLK // 2, FH - FA_H), BF16), vmem((10, BLK // 2, FH - FA_G), BF16),
             vmem((BLK, FH), F32), vmem((TOK, FH), BF16), vmem((TOK, FH), BF16),
             vmem((2, TOK, DC), F32), vmem((2, TOK, DC), BF16),
-            vmem((2, 10, BLK, DC), BF16),
-            vmem((DP, FH), BF16), vmem((FH, DP), BF16), vmem((2, BLK, DC), BF16), vmem((DP, TOK), BF16),
+            vmem((10, BLK, DC), BF16), vmem((10, BLK, FA_D), BF16),
+            vmem((5, BLK, DC - FA_D), BF16), vmem((10, BLK // 2, DC - FA_D), BF16),
+            vmem((DC, FH), BF16), vmem((FH, DP), BF16), vmem((DP, TOK), BF16),
             pltpu.SemaphoreType.DMA((COPIES,)), pltpu.SemaphoreType.DMA((COPIES,)),
-            pltpu.SemaphoreType.DMA((8,)),
+            pltpu.SemaphoreType.DMA((4,)),
         ],
         compiler_params=pltpu.CompilerParams(
-            collective_id=0, has_side_effects=True, vmem_limit_bytes=60 * 1024 * 1024
+            collective_id=0, has_side_effects=True, vmem_limit_bytes=55 * 1024 * 1024
         ),
         cost_estimate=pl.CostEstimate(flops=14_500_000_000, bytes_accessed=12_000_000, transcendentals=400_000),
     )(tokens, weight_in, weight_out, cotangent)

time: 128 us -> 132 us (1.031)
  local copies, waits for them, and re-layouts: 0 us -> 4.08 us
    unnamed x0 -> x8, local copies, waits for them, and re-layouts: none -> 4.08 us
where the time goes in v8:
time: 132 us
  Pallas kernels  127 us (96%)
  local copies, waits for them, and re-layouts  4.08 us (3%)
    pallas_call x1, Pallas kernels, block(): pl.pallas_call(kernel, out_shape=(vmem((BLK, DC), BF16), vmem((BLK, DC),...  122 us
    pallas_call x1, Pallas kernels, local(): pl.pallas_call(hand_over, out_shape=tuple((jax.ShapeDtypeStruct(r.shape,...  4.82 us
    unnamed x8, local copies, waits for them, and re-layouts  4.08 us

profile of v8, /device:TPU:0, one launch (start us, length us, event | category | flops | bytes accessed | tf_op | source)
XLA Modules:
  0.0 131.8 jit_solution(5142167384722053272)
XLA Ops:
  0.6 122.3 %shard_map.75 = (bf16[128,384]{1,0:T(8,128)(2,1)S(1)}, bf16[128,384]{1,0:T(8,128)(2,1)S(1)}, bf16[384,3072]{1,0:T(8,128)(2,1)S(1)}, bf16[3072,384]{1,0:T(8,128)(2,1)S(1)}) custom-call(bf16[128,384]{1,0:T(8,128)(2,1)} %tok_in.1, bf16[384,3072]{1,0:T(8,128)(2,1)} %wi_in.1, bf16[3072,384]{1,0:T(8,128)(2,1)} %wo_in.1, bf16[128,384]{1,0:T(8,128)(2,1)} %cot_in.1), custom_call_target="tpu_custom_call" | custom-call | flops 14499999744 | bytes 12000000 | tf_op jit(solution)/shard_map/pallas_call | solution.py:698
  122.9 0.0 copy-start
  122.9 1.4 %copy-done = bf16[384,3072]{1,0:T(8,128)(2,1)} copy-done((bf16[384,3072]{1,0:T(8,128)(2,1)}, bf16[384,3072]{1,0:T(8,128)(2,1)S(1)}, u32[]{:S(2)}) %copy-start) | copy-done | bytes 2359320
  124.3 0.0 copy-start.1
  124.3 1.4 %copy-done.1 = bf16[3072,384]{1,0:T(8,128)(2,1)} copy-done((bf16[3072,384]{1,0:T(8,128)(2,1)}, bf16[3072,384]{1,0:T(8,128)(2,1)S(1)}, u32[]{:S(2)}) %copy-start.1) | copy-done | bytes 2359320
  125.7 0.0 copy-start.2
  125.7 0.6 copy-done.2
  126.4 0.0 copy-start.3
  126.4 0.6 copy-done.3
  127.0 4.8 %shard_map.76 = (bf16[128,384]{1,0:T(8,128)(2,1)}, bf16[128,384]{1,0:T(8,128)(2,1)}, bf16[384,3072]{1,0:T(8,128)(2,1)}, bf16[3072,384]{1,0:T(8,128)(2,1)}) custom-call(bf16[128,384]{1,0:T(8,128)(2,1)} %copy-done.2, bf16[128,384]{1,0:T(8,128)(2,1)} %copy-done.3, bf16[384,3072]{1,0:T(8,128)(2,1)} %copy-done, bf16[3072,384]{1,0:T(8,128)(2,1)} %copy-done.1), custom_call_target="tpu_custom_call" | custom-call | tf_op jit(solution)/shard_map/pallas_call | solution.py:685
Async XLA Ops:
  122.9 1.4 %copy-start = (bf16[384,3072]{1,0:T(8,128)(2,1)}, bf16[384,3072]{1,0:T(8,128)(2,1)S(1)}, u32[]{:S(2)}) copy-start(bf16[384,3072]{1,0:T(8,128)(2,1)S(1)} %get-tuple-element.10.refs_2_) | copy-start | bytes 7077892
  124.3 1.4 %copy-start.1 = (bf16[3072,384]{1,0:T(8,128)(2,1)}, bf16[3072,384]{1,0:T(8,128)(2,1)S(1)}, u32[]{:S(2)}) copy-start(bf16[3072,384]{1,0:T(8,128)(2,1)S(1)} %get-tuple-element.11.refs_3_) | copy-start | bytes 7077892
  125.7 0.6 copy-start.2
  126.4 0.6 copy-start.3

commit v9 on v8

--- a/solution.py
+++ b/solution.py
@@ -372,12 +372,12 @@
 
 ORDER = (
     "t0", "tp", "t1", "ts0", "c0", "ts1", "hpart0", "tm", "ts-1", "c1", "cs0", "hpart1", "ts2", "hpart-1",
-    "cm", "cs1", "cp", "hpart2", "cs-1", "gpart0", "gpart1", "cs2", "gpart-1", "turn", "gpart2", "hap", "ham",
-    "gam", "hb1", "hb2", "gap", "hay", "hb3", "hbm", "hbp", "gay", "gb3", "gb2", "gb1", "haf", "hbf", "hA0",
-    "hB0", "gaf", "gA0", "hBm", "gbp", "gbm", "hBp", "hA1", "gbf", "gB0", "hAm", "hByp", "ox0", "hAp", "ox1",
-    "hBym", "ox-1", "gA1", "ix0", "gBm", "om0", "om1", "gBp", "om-1", "ox2", "gAp", "go0", "gAm", "ix1",
-    "om2", "or", "gByp", "im0", "gBym", "ix-1", "go1", "odm", "im-1", "ix2", "im1", "odp", "gj0", "im2", "ir",
-    "ie1", "ie2", "ie3", "go", "ody", "idm", "idp", "gi0", "gi", "idy", "odf", "iem", "iep", "ief", "idf",
+    "cs1", "cp", "cs-1", "cm", "hpart2", "gpart0", "gpart1", "cs2", "gpart-1", "gpart2", "hap", "ham", "gam",
+    "hb1", "hb2", "gap", "hb3", "hay", "hbm", "hbp", "gay", "gb2", "gb3", "turn", "gb1", "haf", "hbf", "hA0",
+    "hB0", "gaf", "gbp", "gA0", "hBm", "gbm", "hA1", "hBp", "gbf", "gB0", "hAm", "hAp", "hByp", "ox0", "ox1",
+    "hBym", "ox-1", "gA1", "ix0", "gBm", "om1", "om0", "gBp", "gAp", "om-1", "ox2", "go0", "gAm", "ix1",
+    "om2", "or", "gByp", "gBym", "ix-1", "go1", "ix2", "odp", "odm", "im0", "im-1", "im1", "go", "im2", "ir",
+    "gj0", "ody", "idm", "idp", "ie2", "gi0", "gi", "ie3", "idy", "ie1", "odf", "iem", "iep", "ief", "idf",
 )
 
 
@@ -685,9 +685,10 @@
     return pl.pallas_call(
         hand_over,
         out_shape=tuple(jax.ShapeDtypeStruct(r.shape, r.dtype) for r in results),
-        in_specs=[pl.BlockSpec(memory_space=pltpu.VMEM)] * 4,
+        in_specs=[any_space] * 4,
         out_specs=(any_space,) * 4,
         scratch_shapes=[pltpu.SemaphoreType.DMA((10,))],
+        compiler_params=pltpu.CompilerParams(vmem_limit_bytes=2 * 1024 * 1024),
     )(*results)
 
 

time: 132 us -> 123 us (0.932)
  Pallas kernels: 127 us -> 122 us
  local copies, waits for them, and re-layouts: 4.08 us -> 0 us
    unnamed x8 -> x0, local copies, waits for them, and re-layouts: 4.08 us -> none
    pallas_call x1, Pallas kernels: 4.82 us -> 2.33 us  [local(): pl.pallas_call(hand_over, out_shape=tuple((jax.ShapeDtypeStruct(r.shape,...]
    pallas_call x1, Pallas kernels: 122 us -> 120 us  [block(): pl.pallas_call(kernel, out_shape=(vmem((BLK, DC), BF16), vmem((BLK, DC),...]
where the time goes in v9:
time: 123 us
  Pallas kernels  122 us (99%)
    pallas_call x1, Pallas kernels, block(): pl.pallas_call(kernel, out_shape=(vmem((BLK, DC), BF16), vmem((BLK, DC),...  120 us

profile of v9, /device:TPU:0, one launch (start us, length us, event | category | flops | bytes accessed | tf_op | source)
XLA Modules:
  0.0 123.1 jit_solution(14948090946523769713)
XLA Ops:
  0.6 120.1 %shard_map.75 = (bf16[128,384]{1,0:T(8,128)(2,1)S(1)}, bf16[128,384]{1,0:T(8,128)(2,1)S(1)}, bf16[384,3072]{1,0:T(8,128)(2,1)S(1)}, bf16[3072,384]{1,0:T(8,128)(2,1)S(1)}) custom-call(bf16[128,384]{1,0:T(8,128)(2,1)} %tok_in.1, bf16[384,3072]{1,0:T(8,128)(2,1)} %wi_in.1, bf16[3072,384]{1,0:T(8,128)(2,1)} %wo_in.1, bf16[128,384]{1,0:T(8,128)(2,1)} %cot_in.1), custom_call_target="tpu_custom_call" | custom-call | flops 14499999744 | bytes 12000000 | tf_op jit(solution)/shard_map/pallas_call | solution.py:699
  120.7 2.3 %shard_map.76 = (bf16[128,384]{1,0:T(8,128)(2,1)}, bf16[128,384]{1,0:T(8,128)(2,1)}, bf16[384,3072]{1,0:T(8,128)(2,1)}, bf16[3072,384]{1,0:T(8,128)(2,1)}) custom-call(bf16[128,384]{1,0:T(8,128)(2,1)S(1)} %get-tuple-element.8.refs_0_, bf16[128,384]{1,0:T(8,128)(2,1)S(1)} %get-tuple-element.9.refs_1_, bf16[384,3072]{1,0:T(8,128)(2,1)S(1)} %get-tuple-element.10.refs_2_, ...), custom_call_target="tpu_custom_call" | custom-call | tf_op jit(solution)/shard_map/pallas_call | solution.py:685
